TPU v7x, 128 devices: a whole 4x4x4 slice. The times are simulated.
128 devices in a mesh: tm: 8 (over y_lo, x), slab: 16 (over y_hi, z, core).
Axes of the slice: x: 4, y: 4 (y_hi: 2, y_lo: 2; y = y_hi * 2 + y_lo), z: 4, core: 2. Of those that a mesh axis runs over, the one named last changes fastest.
Arguments:
- u_states: bfloat16 [8, 64, 64, 8, 256], P('tm', None, 'slab'), may hold values from -6 to 6
- lam_points: float32 [8, 64, 64, 8, 256], P('tm', None, 'slab'), may hold values from -6 to 6
- weight: bfloat16 [27, 64, 64], replicated, may hold values from -0.15625 to 0.15625
- bias: float32 [64], replicated, may hold values from -3 to 3
Outputs:
- lam_new: float32 [8, 64, 64, 8, 256], P('tm', None, 'slab')
- grad_w: float32 [27, 64, 64], replicated
- grad_b: float32 [64], replicated
All inputs are finite; a program needn't handle non-finite values.
Results may differ from a plain program's by a relative error of at most 0.0065.
Values may be sent and summed in bfloat16 or wider, within the bound.
No kernel may reach another device: no remote copies, remote signals or barrier semaphores. Data moves between devices by JAX's collectives and lax.ppermute only.
A program may use at most 256 MiB of HBM per device.

v0:
```python
import math

import jax
import jax.numpy as jnp
from jax import lax
from jax.sharding import PartitionSpec as P

step_size = 0.25


def padded_2(x, sides, width):
    for axis, dim in sides:
        devices, length = (lax.axis_size(axis), x.shape[dim])
        up = [(i, (i + 1) % devices) for i in range(devices - 1)]
        down = [(j, i) for i, j in up]
        last = lax.slice_in_dim(x, length - width, length, axis=dim)
        initial = lax.slice_in_dim(x, 0, width, axis=dim)
        before = lax.ppermute(last, axis, up)
        after = lax.ppermute(initial, axis, down)
        x = jnp.concatenate([before, x, after], axis=dim)
    return x


def passed_along(value, axis, steps):
    count = lax.axis_size(axis)
    initial, last = (max(0, -steps), min(count, count - steps))
    return lax.ppermute(value, axis, [(source, source + steps) for source in range(initial, last)])


def columns(widened, z_shift, x_shift, planes):
    channels = widened.shape[0]
    extent_x = widened.shape[2] - 2
    extent_y = widened.shape[3] - 2
    shifted = [
        widened[
            :,
            z_shift : z_shift + planes,
            x_shift : x_shift + extent_x,
            y_shift : y_shift + extent_y,
        ]
        for y_shift in range(3)
    ]
    return jnp.concatenate(shifted, 0).reshape(3 * channels, planes * extent_x * extent_y)


def apply_taps(padded, taps):
    widened = jnp.pad(padded, ((0, 0), (0, 0), (1, 1), (1, 1)))
    planes = padded.shape[1] - 2
    outputs = taps.shape[1]
    running = jnp.zeros((outputs, planes * padded.shape[2] * padded.shape[3]), jnp.float32)
    for z_shift in range(3):
        for x_shift in range(3):
            first_tap = 9 * z_shift + 3 * x_shift
            matrix = (
                taps[first_tap : first_tap + 3]
                .transpose(1, 0, 2)
                .reshape(outputs, 3 * taps.shape[2])
            )
            running = running + jnp.dot(
                matrix,
                columns(widened, z_shift, x_shift, planes),
                preferred_element_type=jnp.float32,
            )
    return running.reshape(outputs, planes, padded.shape[2], padded.shape[3])


def taps_grad(cotangent, padded):
    widened = jnp.pad(padded, ((0, 0), (0, 0), (1, 1), (1, 1)))
    planes = cotangent.shape[1]
    channels = cotangent.shape[0]
    flattened = cotangent.reshape(channels, -1)
    blocks = []
    for z_shift in range(3):
        for x_shift in range(3):
            product = lax.dot_general(
                flattened,
                columns(widened, z_shift, x_shift, planes),
                (((1,), (1,)), ((), ())),
                preferred_element_type=jnp.float32,
            )
            blocks.append(product.reshape(channels, 3, padded.shape[0]).transpose(1, 0, 2))
    return jnp.concatenate(blocks, 0)


def restrict(field):
    shaped = field.reshape(
        field.shape[0], field.shape[1], field.shape[2] // 2, 2, field.shape[3] // 2, 2
    )
    return jnp.mean(shaped, axis=(3, 5))


def prolong(field):
    return jnp.repeat(jnp.repeat(field, 2, axis=2), 2, axis=3)


def transposed(cotangent, flipped):
    padded = padded_2(cotangent, (("slab", 1),), 1)
    return apply_taps(padded, flipped)


def on_device(u_states, lam_points, weight, bias):
    state_zero = u_states[0]
    adjoint = lam_points[0]
    depth_cells = state_zero.shape[1]
    offset = bias[:, None, None, None]
    flipped = weight[::-1].transpose(0, 2, 1)
    zero_pad = padded_2(state_zero, (("slab", 1),), 1)
    tanh_zero = jnp.tanh(apply_taps(zero_pad, weight) + offset)
    state_one = (state_zero.astype(jnp.float32) + step_size * tanh_zero).astype(jnp.bfloat16)
    one_pad = padded_2(state_one, (("slab", 1),), 1)
    sens_zero = 1.0 - tanh_zero * tanh_zero
    tanh_one = jnp.tanh(apply_taps(one_pad, weight) + offset)
    sens_one = 1.0 - tanh_one * tanh_one
    cot_one = (sens_one * adjoint).astype(jnp.bfloat16)
    middle = adjoint + step_size * transposed(cot_one, flipped)
    cot_zero = (sens_zero * middle).astype(jnp.bfloat16)
    fine_back = middle + step_size * transposed(cot_zero, flipped)
    weight_grad = taps_grad(cot_zero, zero_pad) + taps_grad(cot_one, one_pad)
    bias_grad = jnp.sum(cot_zero.astype(jnp.float32) + cot_one.astype(jnp.float32), axis=(1, 2, 3))
    diagonal = jnp.diagonal(weight[13]).astype(jnp.float32)
    factor = 1.0 + 2.0 * step_size * diagonal[:, None, None, None] * restrict(sens_zero)
    lower, factor_prev = passed_along((restrict(fine_back), factor), "tm", 1)
    rest = lower - restrict(adjoint)

    def sweep_once(counter, value):
        return factor_prev * passed_along(value, "tm", 1) + rest

    correction = lax.fori_loop(0, lax.axis_size("tm") - 1, sweep_once, rest)
    updated = adjoint + prolong(correction)
    weight_total, bias_total = lax.psum((weight_grad, bias_grad), ("tm", "slab"))
    grad_scale = step_size / math.sqrt(
        2
        * lax.axis_size("tm")
        * depth_cells
        * lax.axis_size("slab")
        * state_zero.shape[2]
        * state_zero.shape[3]
    )
    return (updated[None], weight_total * grad_scale, bias_total * grad_scale)


def solution(mesh):
    in_specs = (P("tm", None, "slab", None, None), P("tm", None, "slab", None, None), P(), P())
    out_specs = (P("tm", None, "slab", None, None), P(), P())
    return jax.shard_map(
        on_device, mesh=mesh, in_specs=in_specs, out_specs=out_specs, check_vma=False
    )
```

profile of v0, /device:TPU:24, one launch (start us, length us, event | category | flops | bytes accessed | tf_op | source)
XLA Modules:
  0.0 772.6 jit_solution(14880145000830984706)
XLA Ops:
  10.3 7.3 collective-permute-start.2
  24.1 5.0 fusion.21
  29.1 9.0 %fusion.96 = (bf16[64,4,8,256]{3,2,1,0:T(8,128)(2,1)S(1)}, bf16[64,4,8,256]{3,2,1,0:T(8,128)(2,1)S(1)}, bf16[64,4,8,256]{3,2,1,0:T(8,128)(2,1)S(1)}, bf16[64,4,8...) fusion(bf16[64,6,10,258]{3,2,1,0:T(8,128)(2,1)S(1)} %fusion.21), kind=kLoop, calls=%fused_computation.218 | loop fusion | bytes 39845888 | tf_op jit(solution)/shard_map/slice | solution.py:35
  38.0 3.7 fusion.97
  79.5 10.9 %convolution_add_fusion.28 = f32[8192,64]{0,1:T(8,128)S(1)} fusion(f32[8192,64]{0,1:T(8,128)S(1)} %convolution_add_fusion.29, bf16[64,192]{0,1:T(8,128)(2,1)S(1)} %bitcast.599, bf16[64,8192]{1,0:T(8,128)(2,1)S(1)} %bitcast.564, bf16[64,8192]{1,0:T(8,128)(2,1)S(1)} %copy-done.89, bf16[64,8192]{1,0:T(8,128)(2,1)S(1)} %bitcast.563), kind=kOutput, calls=%fused_computation.40 | convolution fusion | flops 211288064 | bytes 7364608 | tf_op jit(solution)/shard_map/dot_general | solution.py:59
  99.8 7.3 collective-permute-start.4
  115.6 3.8 copy.78
  119.4 6.8 copy.79
  126.2 5.8 fusion.19
  132.0 8.9 %fusion.94 = (bf16[64,4,8,256]{3,2,1,0:T(8,128)(2,1)S(1)}, bf16[64,4,8,256]{3,2,1,0:T(8,128)(2,1)S(1)}, bf16[64,4,8,256]{3,2,1,0:T(8,128)(2,1)S(1)}, bf16[64,4,8...) fusion(bf16[64,6,10,258]{3,2,1,0:T(8,128)(2,1)S(1)} %fusion.19), kind=kLoop, calls=%fused_computation.216 | loop fusion | bytes 39845888 | tf_op jit(solution)/shard_map/slice | solution.py:35
  153.7 4.0 copy.103
  158.1 3.9 copy.102
  162.1 4.5 fusion.31
  194.0 7.3 collective-permute-start.6
  205.9 5.9 dot_general.284
  211.8 6.1 dot_general.286
  221.4 6.0 dot_general.292
  230.8 6.0 dot_general.296
  240.2 6.0 dot_general.290
  255.1 5.9 dot_general.302
  260.9 6.0 dot_general.304
  270.4 5.9 dot_general.308
  276.2 6.0 dot_general.310
  285.7 6.0 dot_general.314
  295.9 9.3 %select_maximum_fusion.2 = bf16[64,6,10,258]{3,2,1,0:T(8,128)(2,1)S(1)} fusion(bf16[64,1,8,256]{3,2,1,0:T(8,128)(2,1)} %collective-permute-done.6, bf16[64,4,8,256]{3,2,1,0:T(8,128)(2,1)} %copy-done.40, bf16[64,1,8,256]{3,2,1,0:T(8,128)(2,1)S(1)} %collective-permute-done.5), kind=kLoop, calls=%fused_computation.46 | loop fusion | flops 18823680 | bytes 3554304 | tf_op jit(solution)/shard_map/concatenate | solution.py:20
  305.3 8.9 %fusion.92 = (bf16[64,4,8,256]{3,2,1,0:T(8,128)(2,1)S(1)}, bf16[64,4,8,256]{3,2,1,0:T(8,128)(2,1)S(1)}, bf16[64,4,8,256]{3,2,1,0:T(8,128)(2,1)S(1)}, bf16[64,4,8...) fusion(bf16[64,6,10,258]{3,2,1,0:T(8,128)(2,1)S(1)} %select_max, ...), kind=kLoop, calls=%fused_computation.214 | loop fusion | bytes 39845888 | tf_op jit(solution)/shard_map/slice | solution.py:35
  331.0 4.7 fusion.27
  335.7 4.3 copy.111
  364.7 7.3 collective-permute-start.8
  372.0 3.9 copy.74
  375.9 4.0 fusion.59
  411.5 5.8 select_maximum_fusion
  417.3 9.0 %fusion.90 = (bf16[64,4,8,256]{3,2,1,0:T(8,128)(2,1)S(1)}, bf16[64,4,8,256]{3,2,1,0:T(8,128)(2,1)S(1)}, bf16[64,4,8,256]{3,2,1,0:T(8,128)(2,1)S(1)}, bf16[64,4,8...) fusion(bf16[64,6,10,258]{3,2,1,0:T(8,128)(2,1)S(1)} %select_max, ...), kind=kLoop, calls=%fused_computation.212 | loop fusion | bytes 39845888 | tf_op jit(solution)/shard_map/slice | solution.py:35
  426.3 3.6 fusion.91
  443.4 5.1 fusion.23
  469.2 11.6 %fusion.88 = (f32[64,4,4,128]{0,3,2,1:T(8,128)S(1)}, f32[64,4,4,128]{0,3,2,1:T(8,128)S(1)}) fusion(f32[64,4,4,2,128,2]{0,5,4,3,2,1:T(2,128)} %bitcast.532, f32[64,4,4,2,128,2]{0,5,4,3,2,1:T(2,128)} %bitcast.534, f32[64,4,4,2,128,2]{0,5,4,3,2,1:T(2,128)} %bitcast.533), kind=kLoop, calls=%fused_computation.211 | loop fusion | flops 1835008 | bytes 7340032 | tf_op jit(solution)/shard_map/reduce_sum | solution.py:89
  485.4 3.9 fusion.60
  493.3 62.2 %psum.15 = f32[64]{0:T(128)S(1)} all-reduce(f32[64]{0:T(128)S(1)} %copy-done.122), channel_id=1, replica_groups=mesh['tm'=8,'slab'=16] {'tm','slab'}, use_global_device_ids=true, to_apply=%region_7.8 | all-reduce | flops 64 | bytes 512 | tf_op jit(solution)/shard_map/psum | solution.py:130
  555.9 79.4 %all-reduce.6.cloned.1.call-done = f32[27,64,64]{2,1,0:T(8,128)} async-done(((f32[27,64,64]{2,1,0:T(8,128)}), f32[27,64,64]{2,1,0:T(8,128)}) %all-reduce.6.cloned.1.call-update) | async-done | bytes 442384 | tf_op jit(solution)/shard_map/psum | solution.py:130
  641.7 113.3 %while.10 = (s32[]{:T(128)}, f32[64,4,4,128]{3,2,1,0:T(4,128)S(1)}, f32[64,4,4,128]{3,2,1,0:T(4,128)S(1)}, f32[64,4,4,128]{3,2,1,0:T(4,128)S(1)}, s32[]{:T(128)}) while((s32[]{:T(128)}, f32[64,4,4,128]{3,2,1,0:T(4,128)S(1)}, f32[64,4,4,128]{3,2,1,0:T(4,128)S(1)}, f32[64,4,4,128]{3,2,1,0:T(4,128)S(1)}, s32[]{:T(128)}) %tuple.152), condition=%wide.region_4.5_spmd, body=%wide.region_3.4_spmd.sunk | while | flops 262146 | bytes 4194405 | solution.py:128
  644.8 15.6 %collective-permute-done = f32[64,4,4,128]{3,2,1,0:T(4,128)S(1)} collective-permute-done((f32[64,4,4,128]{3,2,1,0:T(4,128)S(1)}, f32[64,4,4,128]{3,2,1,0:T(4,128)S(1)}, u32[]{:S(2)}, u32[]{:S(2)}) %collective-permute-start) | collective-permute-done | bytes 524320 | tf_op jit(solution)/shard_map/while/body/eval_jaxpr/ppermute | solution.py:27
  662.5 15.9 %collective-permute-done = f32[64,4,4,128]{3,2,1,0:T(4,128)S(1)} collective-permute-done((f32[64,4,4,128]{3,2,1,0:T(4,128)S(1)}, f32[64,4,4,128]{3,2,1,0:T(4,128)S(1)}, u32[]{:S(2)}, u32[]{:S(2)}) %collective-permute-start) | collective-permute-done | bytes 524320 | tf_op jit(solution)/shard_map/while/body/eval_jaxpr/ppermute | solution.py:27
  680.5 15.1 %collective-permute-done = f32[64,4,4,128]{3,2,1,0:T(4,128)S(1)} collective-permute-done((f32[64,4,4,128]{3,2,1,0:T(4,128)S(1)}, f32[64,4,4,128]{3,2,1,0:T(4,128)S(1)}, u32[]{:S(2)}, u32[]{:S(2)}) %collective-permute-start) | collective-permute-done | bytes 524320 | tf_op jit(solution)/shard_map/while/body/eval_jaxpr/ppermute | solution.py:27
  697.6 14.2 %collective-permute-done = f32[64,4,4,128]{3,2,1,0:T(4,128)S(1)} collective-permute-done((f32[64,4,4,128]{3,2,1,0:T(4,128)S(1)}, f32[64,4,4,128]{3,2,1,0:T(4,128)S(1)}, u32[]{:S(2)}, u32[]{:S(2)}) %collective-permute-start) | collective-permute-done | bytes 524320 | tf_op jit(solution)/shard_map/while/body/eval_jaxpr/ppermute | solution.py:27
  713.8 13.3 %collective-permute-done = f32[64,4,4,128]{3,2,1,0:T(4,128)S(1)} collective-permute-done((f32[64,4,4,128]{3,2,1,0:T(4,128)S(1)}, f32[64,4,4,128]{3,2,1,0:T(4,128)S(1)}, u32[]{:S(2)}, u32[]{:S(2)}) %collective-permute-start) | collective-permute-done | bytes 524320 | tf_op jit(solution)/shard_map/while/body/eval_jaxpr/ppermute | solution.py:27
  729.1 12.3 %collective-permute-done = f32[64,4,4,128]{3,2,1,0:T(4,128)S(1)} collective-permute-done((f32[64,4,4,128]{3,2,1,0:T(4,128)S(1)}, f32[64,4,4,128]{3,2,1,0:T(4,128)S(1)}, u32[]{:S(2)}, u32[]{:S(2)}) %collective-permute-start) | collective-permute-done | bytes 524320 | tf_op jit(solution)/shard_map/while/body/eval_jaxpr/ppermute | solution.py:27
  743.5 11.4 %collective-permute-done = f32[64,4,4,128]{3,2,1,0:T(4,128)S(1)} collective-permute-done((f32[64,4,4,128]{3,2,1,0:T(4,128)S(1)}, f32[64,4,4,128]{3,2,1,0:T(4,128)S(1)}, u32[]{:S(2)}, u32[]{:S(2)}) %collective-permute-start) | collective-permute-done | bytes 524320 | tf_op jit(solution)/shard_map/while/body/eval_jaxpr/ppermute | solution.py:27
  760.8 4.5 copy.87
  (444 shorter events, 283.0 us)
Async XLA Ops:
  7.2 16.9 %copy-start.33 = (bf16[1,64,4,8,256]{4,3,2,1,0:T(8,128)(2,1)S(1)}, bf16[1,64,4,8,256]{4,3,2,1,0:T(8,128)(2,1)}, u32[]{:S(2)}) copy-start(bf16[1,64,4,8,256]{4,3,2,1,0:T(8,128)(2,1)} %param.6) | copy-start | bytes 3145732
  7.2 628.1 %all-reduce.6.cloned.1.call-start = ((), (), s32[]{:S(2)}) async-start(), calls=%async_computation | async-start | bytes 1769472 | tf_op jit(solution)/shard_map/psum | solution.py:130
  8.4 15.7 %collective-permute-start.1 = (bf16[64,1,8,256]{3,2,1,0:T(8,128)(2,1)S(1)}, bf16[64,1,8,256]{3,2,1,0:T(8,128)(2,1)S(1)}, u32[]{:S(2)}, u32[]{:S(2)}) collective-permute-start(bf16[64,1,8,256]{3,2,1,0:T(8,128)(2,1)S(1)} %get-tuple-element.177), channel_id=1, source_target_pairs={{0,1},{1,2},{2,3},{3,4},{4,5},{5,6},{6,7},{7,8},{8,9},{9,10},{10,1... | collective-permute-start | bytes 786440 | tf_op jit(solution)/shard_map/ppermute | solution.py:18
  10.3 13.8 %collective-permute-start.2 = (bf16[64,1,8,256]{3,2,1,0:T(8,128)(2,1)S(1)}, bf16[64,1,8,256]{3,2,1,0:T(8,128)(2,1)S(1)}, u32[]{:S(2)}, u32[]{:S(2)}) collective-permute-start(bf16[64,1,8,256]{3,2,1,0:T(8,128)(2,1)S(1)} %get-tuple-element.178), channel_id=1, source_target_pairs={{1,0},{2,1},{3,2},{4,3},{5,4},{6,5},{7,6},{8,7},{9,8},{10,9},{11,1... | collective-permute-start | bytes 786440 | tf_op jit(solution)/shard_map/ppermute | solution.py:19
  21.8 53.6 %copy-start.115 = (bf16[64,3,64]{0,2,1:T(8,128)(2,1)}, bf16[64,3,64]{0,2,1:T(8,128)(2,1)S(1)}, u32[]{:S(2)}) copy-start(bf16[64,3,64]{0,2,1:T(8,128)(2,1)S(1)} %copy.65) | copy-start | bytes 73732
  21.9 54.2 %copy-start.111 = (bf16[64,3,64]{0,2,1:T(8,128)(2,1)}, bf16[64,3,64]{0,2,1:T(8,128)(2,1)S(1)}, u32[]{:S(2)}) copy-start(bf16[64,3,64]{0,2,1:T(8,128)(2,1)S(1)} %copy.66) | copy-start | bytes 73732
  22.0 54.9 %copy-start.109 = (bf16[64,3,64]{0,2,1:T(8,128)(2,1)}, bf16[64,3,64]{0,2,1:T(8,128)(2,1)S(1)}, u32[]{:S(2)}) copy-start(bf16[64,3,64]{0,2,1:T(8,128)(2,1)S(1)} %copy.67) | copy-start | bytes 73732
  22.1 55.5 %copy-start.107 = (bf16[64,3,64]{0,2,1:T(8,128)(2,1)}, bf16[64,3,64]{0,2,1:T(8,128)(2,1)S(1)}, u32[]{:S(2)}) copy-start(bf16[64,3,64]{0,2,1:T(8,128)(2,1)S(1)} %copy.68) | copy-start | bytes 73732
  22.2 56.2 %copy-start.117 = (bf16[64,3,64]{0,2,1:T(8,128)(2,1)}, bf16[64,3,64]{0,2,1:T(8,128)(2,1)S(1)}, u32[]{:S(2)}) copy-start(bf16[64,3,64]{0,2,1:T(8,128)(2,1)S(1)} %copy.69) | copy-start | bytes 73732
  22.4 68.1 %copy-start.105 = (bf16[64,3,64]{0,2,1:T(8,128)(2,1)}, bf16[64,3,64]{0,2,1:T(8,128)(2,1)S(1)}, u32[]{:S(2)}) copy-start(bf16[64,3,64]{0,2,1:T(8,128)(2,1)S(1)} %copy.70) | copy-start | bytes 73732
  45.2 25.6 %copy-start.26 = (bf16[192,4,8,256]{3,2,1,0:T(8,128)(2,1)}, bf16[192,4,8,256]{3,2,1,0:T(8,128)(2,1)S(1)}, u32[]{:S(2)}) copy-start(bf16[192,4,8,256]{3,2,1,0:T(8,128)(2,1)S(1)} %get-tuple-element.160) | copy-start | bytes 9437188
  45.2 4.4 copy-start.70
  50.4 22.7 %copy-start.16 = (bf16[192,4,8,256]{3,2,1,0:T(8,128)(2,1)}, bf16[192,4,8,256]{3,2,1,0:T(8,128)(2,1)S(1)}, u32[]{:S(2)}) copy-start(bf16[192,4,8,256]{3,2,1,0:T(8,128)(2,1)S(1)} %get-tuple-element.199) | copy-start | bytes 9437188
  95.4 11.7 %copy-start.86 = (bf16[27,64,64]{2,1,0:T(8,128)(2,1)S(1)}, bf16[27,64,64]{2,1,0:T(8,128)(2,1)}, u32[]{:S(2)}) copy-start(bf16[27,64,64]{2,1,0:T(8,128)(2,1)} %param.8) | copy-start | bytes 663556
  95.4 11.7 %copy-start = (f32[1,64,4,8,256]{4,3,2,1,0:T(8,128)S(1)}, f32[1,64,4,8,256]{4,3,2,1,0:T(8,128)}, u32[]{:S(2)}) copy-start(f32[1,64,4,8,256]{4,3,2,1,0:T(8,128)} %param.7) | copy-start | bytes 6291460
  97.9 28.2 %collective-permute-start.3 = (bf16[64,1,8,256]{3,2,1,0:T(8,128)(2,1)}, bf16[64,1,8,256]{3,2,1,0:T(8,128)(2,1)S(1)}, u32[]{:S(2)}, u32[]{:S(2)}) collective-permute-start(bf16[64,1,8,256]{3,2,1,0:T(8,128)(2,1)} %get-tuple-element.175), channel_id=1, source_target_pairs={{0,1},{1,2},{2,3},{3,4},{4,5},{5,6},{6,7},{7,8},{8,9},{9,10},{10,1... | collective-permute-start | bytes 786440 | tf_op jit(solution)/shard_map/ppermute | solution.py:18
  99.8 26.3 %collective-permute-start.4 = (bf16[64,1,8,256]{3,2,1,0:T(8,128)(2,1)}, bf16[64,1,8,256]{3,2,1,0:T(8,128)(2,1)}, u32[]{:S(2)}, u32[]{:S(2)}) collective-permute-start(bf16[64,1,8,256]{3,2,1,0:T(8,128)(2,1)} %get-tuple-element.176), channel_id=1, source_target_pairs={{1,0},{2,1},{3,2},{4,3},{5,4},{6,5},{7,6},{8,7},{9,8},{10,9},{11,1... | collective-permute-start | bytes 786440 | tf_op jit(solution)/shard_map/ppermute | solution.py:19
  119.4 6.8 copy-start.39
  166.5 7.1 copy-start.30
  166.6 7.8 %copy-start.29 = (bf16[192,4,8,256]{3,2,1,0:T(8,128)(2,1)}, bf16[192,4,8,256]{3,2,1,0:T(8,128)(2,1)S(1)}, u32[]{:S(2)}) copy-start(bf16[192,4,8,256]{3,2,1,0:T(8,128)(2,1)S(1)} %get-tuple-element.173) | copy-start | bytes 9437188
  166.6 10.1 %copy-start.28 = (bf16[192,4,8,256]{3,2,1,0:T(8,128)(2,1)}, bf16[192,4,8,256]{3,2,1,0:T(8,128)(2,1)S(1)}, u32[]{:S(2)}) copy-start(bf16[192,4,8,256]{3,2,1,0:T(8,128)(2,1)S(1)} %get-tuple-element.172) | copy-start | bytes 9437188
  166.6 4.2 copy-start.79
  189.6 11.7 %copy-start.62 = (f32[64,4,4,2,128,2]{4,0,5,3,2,1:T(8,128)S(1)}, f32[64,4,4,2,128,2]{4,0,5,3,2,1:T(8,128)}, u32[]{:S(2)}) copy-start(f32[64,4,4,2,128,2]{4,0,5,3,2,1:T(8,128)} %copy.79) | copy-start | bytes 6291460
  191.1 11.4 %copy-start.19 = (bf16[192,4,8,256]{3,2,1,0:T(8,128)(2,1)S(1)}, bf16[192,4,8,256]{3,2,1,0:T(8,128)(2,1)}, u32[]{:S(2)}) copy-start(bf16[192,4,8,256]{3,2,1,0:T(8,128)(2,1)} %copy-done.18) | copy-start | bytes 9437188
  192.0 103.2 %collective-permute-start.5 = (bf16[64,1,8,256]{3,2,1,0:T(8,128)(2,1)}, bf16[64,1,8,256]{3,2,1,0:T(8,128)(2,1)S(1)}, u32[]{:S(2)}, u32[]{:S(2)}) collective-permute-start(bf16[64,1,8,256]{3,2,1,0:T(8,128)(2,1)} %get-tuple-element.170), channel_id=1, source_target_pairs={{0,1},{1,2},{2,3},{3,4},{4,5},{5,6},{6,7},{7,8},{8,9},{9,10},{10,1... | collective-permute-start | bytes 786440 | tf_op jit(solution)/shard_map/ppermute | solution.py:18
  194.0 101.2 %collective-permute-start.6 = (bf16[64,1,8,256]{3,2,1,0:T(8,128)(2,1)}, bf16[64,1,8,256]{3,2,1,0:T(8,128)(2,1)}, u32[]{:S(2)}, u32[]{:S(2)}) collective-permute-start(bf16[64,1,8,256]{3,2,1,0:T(8,128)(2,1)} %get-tuple-element.171), channel_id=1, source_target_pairs={{1,0},{2,1},{3,2},{4,3},{5,4},{6,5},{7,6},{8,7},{9,8},{10,9},{11,1... | collective-permute-start | bytes 786440 | tf_op jit(solution)/shard_map/ppermute | solution.py:19
  211.8 6.1 copy-start.21
  221.3 6.0 copy-start.24
  230.8 6.0 copy-start.17
  240.2 6.0 copy-start.123
  240.2 11.4 %copy-start.15 = (bf16[192,4,8,256]{3,2,1,0:T(8,128)(2,1)S(1)}, bf16[192,4,8,256]{3,2,1,0:T(8,128)(2,1)}, u32[]{:S(2)}) copy-start(bf16[192,4,8,256]{3,2,1,0:T(8,128)(2,1)} %copy-done.14) | copy-start | bytes 9437188
  248.2 243.7 %collective-permute-start.10 = (f32[64,4,4,128]{3,0,2,1:T(8,128)}, f32[64,4,4,128]{3,0,2,1:T(8,128)}, u32[]{:S(2)}, u32[]{:S(2)}) collective-permute-start(f32[64,4,4,128]{3,0,2,1:T(8,128)} %multiply_add_fusion.1), channel_id=1, source_target_pairs={{0,16},{16,32},{32,48},{48,64},{64,80},{80,96},{96,112},{1,17},{17... | collective-permute-start | bytes 1572872 | tf_op jit(solution)/shard_map/ppermute | solution.py:27
  260.9 6.0 copy-start.12
  276.2 6.0 copy-start.9
  285.7 6.0 copy-start.7
  335.7 4.3 copy-start.71
  335.7 4.3 copy-start.72
  335.7 4.3 copy-start.73
  362.8 47.8 %collective-permute-start.7 = (bf16[64,1,8,256]{3,2,1,0:T(8,128)(2,1)}, bf16[64,1,8,256]{3,2,1,0:T(8,128)(2,1)S(1)}, u32[]{:S(2)}, u32[]{:S(2)}) collective-permute-start(bf16[64,1,8,256]{3,2,1,0:T(8,128)(2,1)} %get-tuple-element.165), channel_id=1, source_target_pairs={{0,1},{1,2},{2,3},{3,4},{4,5},{5,6},{6,7},{7,8},{8,9},{9,10},{10,1... | collective-permute-start | bytes 786440 | tf_op jit(solution)/shard_map/ppermute | solution.py:18
  364.7 45.9 %collective-permute-start.8 = (bf16[64,1,8,256]{3,2,1,0:T(8,128)(2,1)}, bf16[64,1,8,256]{3,2,1,0:T(8,128)(2,1)}, u32[]{:S(2)}, u32[]{:S(2)}) collective-permute-start(bf16[64,1,8,256]{3,2,1,0:T(8,128)(2,1)} %get-tuple-element.166), channel_id=1, source_target_pairs={{1,0},{2,1},{3,2},{4,3},{5,4},{6,5},{7,6},{8,7},{9,8},{10,9},{11,1... | collective-permute-start | bytes 786440 | tf_op jit(solution)/shard_map/ppermute | solution.py:19
  482.0 155.5 %collective-permute-start.9 = (f32[64,4,4,128]{3,0,2,1:T(8,128)}, f32[64,4,4,128]{3,0,2,1:T(8,128)}, u32[]{:S(2)}, u32[]{:S(2)}) collective-permute-start(f32[64,4,4,128]{3,0,2,1:T(8,128)} %copy.76), channel_id=1, source_target_pairs={{0,16},{16,32},{32,48},{48,64},{64,80},{80,96},{96,112},{1,17},{17... | collective-permute-start | bytes 1572872 | tf_op jit(solution)/shard_map/ppermute | solution.py:27
  641.7 18.7 %collective-permute-start = (f32[64,4,4,128]{3,2,1,0:T(4,128)S(1)}, f32[64,4,4,128]{3,2,1,0:T(4,128)S(1)}, u32[]{:S(2)}, u32[]{:S(2)}) collective-permute-start(f32[64,4,4,128]{3,2,1,0:T(4,128)S(1)} %get-tuple-element.235), channel_id=1, source_target_pairs={{0,16},{16,32},{32,48},{48,64},{64,80},{80,96},{96,112},{1,17},{17... | collective-permute-start | bytes 1572872 | tf_op jit(solution)/shard_map/while/body/eval_jaxpr/ppermute | solution.py:27
  660.5 17.9 %collective-permute-start = (f32[64,4,4,128]{3,2,1,0:T(4,128)S(1)}, f32[64,4,4,128]{3,2,1,0:T(4,128)S(1)}, u32[]{:S(2)}, u32[]{:S(2)}) collective-permute-start(f32[64,4,4,128]{3,2,1,0:T(4,128)S(1)} %get-tuple-element.235), channel_id=1, source_target_pairs={{0,16},{16,32},{32,48},{48,64},{64,80},{80,96},{96,112},{1,17},{17... | collective-permute-start | bytes 1572872 | tf_op jit(solution)/shard_map/while/body/eval_jaxpr/ppermute | solution.py:27
  678.5 17.0 %collective-permute-start = (f32[64,4,4,128]{3,2,1,0:T(4,128)S(1)}, f32[64,4,4,128]{3,2,1,0:T(4,128)S(1)}, u32[]{:S(2)}, u32[]{:S(2)}) collective-permute-start(f32[64,4,4,128]{3,2,1,0:T(4,128)S(1)} %get-tuple-element.235), channel_id=1, source_target_pairs={{0,16},{16,32},{32,48},{48,64},{64,80},{80,96},{96,112},{1,17},{17... | collective-permute-start | bytes 1572872 | tf_op jit(solution)/shard_map/while/body/eval_jaxpr/ppermute | solution.py:27
  695.7 16.1 %collective-permute-start = (f32[64,4,4,128]{3,2,1,0:T(4,128)S(1)}, f32[64,4,4,128]{3,2,1,0:T(4,128)S(1)}, u32[]{:S(2)}, u32[]{:S(2)}) collective-permute-start(f32[64,4,4,128]{3,2,1,0:T(4,128)S(1)} %get-tuple-element.235), channel_id=1, source_target_pairs={{0,16},{16,32},{32,48},{48,64},{64,80},{80,96},{96,112},{1,17},{17... | collective-permute-start | bytes 1572872 | tf_op jit(solution)/shard_map/while/body/eval_jaxpr/ppermute | solution.py:27
  711.9 15.2 %collective-permute-start = (f32[64,4,4,128]{3,2,1,0:T(4,128)S(1)}, f32[64,4,4,128]{3,2,1,0:T(4,128)S(1)}, u32[]{:S(2)}, u32[]{:S(2)}) collective-permute-start(f32[64,4,4,128]{3,2,1,0:T(4,128)S(1)} %get-tuple-element.235), channel_id=1, source_target_pairs={{0,16},{16,32},{32,48},{48,64},{64,80},{80,96},{96,112},{1,17},{17... | collective-permute-start | bytes 1572872 | tf_op jit(solution)/shard_map/while/body/eval_jaxpr/ppermute | solution.py:27
  727.2 14.3 %collective-permute-start = (f32[64,4,4,128]{3,2,1,0:T(4,128)S(1)}, f32[64,4,4,128]{3,2,1,0:T(4,128)S(1)}, u32[]{:S(2)}, u32[]{:S(2)}) collective-permute-start(f32[64,4,4,128]{3,2,1,0:T(4,128)S(1)} %get-tuple-element.235), channel_id=1, source_target_pairs={{0,16},{16,32},{32,48},{48,64},{64,80},{80,96},{96,112},{1,17},{17... | collective-permute-start | bytes 1572872 | tf_op jit(solution)/shard_map/while/body/eval_jaxpr/ppermute | solution.py:27
  741.6 13.3 %collective-permute-start = (f32[64,4,4,128]{3,2,1,0:T(4,128)S(1)}, f32[64,4,4,128]{3,2,1,0:T(4,128)S(1)}, u32[]{:S(2)}, u32[]{:S(2)}) collective-permute-start(f32[64,4,4,128]{3,2,1,0:T(4,128)S(1)} %get-tuple-element.235), channel_id=1, source_target_pairs={{0,16},{16,32},{32,48},{48,64},{64,80},{80,96},{96,112},{1,17},{17... | collective-permute-start | bytes 1572872 | tf_op jit(solution)/shard_map/while/body/eval_jaxpr/ppermute | solution.py:27
  (94 other events, 196.3 us)
Sparse Core Ops, SparseCore 0:
  492.0 143.2 all-reduce.5
where the time goes:
time: 785 us; the launch traced here: 773 us
  local copies, waits for them, and re-layouts  303 us (39%)
  waiting for transfers between devices  177 us (23%)
  other arithmetic  81.8 us (10%)
  matrix products  73.9 us (9%)
  blocking collectives  62.2 us (8%)
  starting transfers between devices  58.2 us (7%)
  between operations  16.5 us (2%)
    unnamed x292, local copies, waits for them, and re-layouts  129 us
    ppermute x9, waiting for transfers between devices, passed_along(): lax.ppermute(value, axis, [(source, source + steps) for source in range(i...  97.8 us
    dot_general x18, local copies, waits for them, and re-layouts, taps_grad(): lax.dot_general(flattened, columns(widened, z_shift, x_shift, planes), ((...  87.3 us
    psum x1, waiting for transfers between devices, on_device(): lax.psum((weight_grad, bias_grad), ('tm', 'slab'))  79.4 us
    psum x1, blocking collectives, on_device(): lax.psum((weight_grad, bias_grad), ('tm', 'slab'))  62.2 us
    slice x8, local copies, waits for them, and re-layouts, columns(): widened[:, z_shift:z_shift + planes, x_shift:x_shift + extent_x, y_shift:...  50.2 us
    dot_general x36, matrix products, apply_taps(): jnp.dot(matrix, columns(widened, z_shift, x_shift, planes), preferred_ele...  38.6 us
    dot_general x18, matrix products, taps_grad(): lax.dot_general(flattened, columns(widened, z_shift, x_shift, planes), ((...  35.3 us
  transfers between devices with their start and end apart: 18, of which 8 were waited for; matrix products, arithmetic and copies ran while one was open for 38% of the time, Pallas kernels for 0%

commit v1 on v0

v1 whole, which is shorter than its diff:
```python
import functools
import math

import jax
import jax.numpy as jnp
from jax import lax
from jax.experimental import pallas as pl
from jax.experimental.pallas import tpu as pltpu
from jax.sharding import PartitionSpec as P

f32, bf16 = jnp.float32, jnp.bfloat16
STEP = 0.25
VMEM_LIMIT = 56 * 2**20
PARAMS = pltpu.CompilerParams(vmem_limit_bytes=VMEM_LIMIT)


def shifts(value):
    lane = lax.broadcasted_iota(jnp.int32, value.shape, 1)
    zero = jnp.zeros((), value.dtype)
    left = jnp.where(lane == 0, zero, pltpu.roll(value, 1, 1))
    right = jnp.where(lane == 255, zero, pltpu.roll(value, 255, 1))
    return left, right


def put(wide, plane, row, pair, value):
    count = value.shape[0]
    left, right = shifts(value)
    base = plane * 384 + row
    cols = slice(pair * 256, pair * 256 + 256)
    wide[pl.ds(base, count), cols] = left
    wide[pl.ds(base + 128, count), cols] = value
    wide[pl.ds(base + 256, count), cols] = right


def to_rows(source, z, turn):
    value = source[:, z].astype(f32).reshape(512, 256)
    turn[0] = value[:, :128]
    turn[1] = value[:, 128:]


def row_of(turn, x):
    return jnp.concatenate([turn[half, pl.ds(x, 64, stride=8), :] for half in range(2)], 1)


def pair_of(turn, pair):
    return jnp.concatenate([row_of(turn, 2 * pair), row_of(turn, 2 * pair + 1)], 0)


def products(matrix, wide, z):
    base = pl.multiple_of(z * 384, 384)
    return [
        jnp.dot(
            matrix[...],
            wide[pl.ds(base, 1152), pair * 256 : pair * 256 + 256],
            preferred_element_type=f32,
        )
        for pair in range(4)
    ]


def combined(parts, pair):
    low, high = parts[pair][0:64], parts[pair][64:128]
    if pair > 0:
        low = low + parts[pair - 1][192:256]
    if pair < 3:
        high = high + parts[pair + 1][128:192]
    return jnp.concatenate([low, high], 0)


def averaging():
    fine = lax.broadcasted_iota(jnp.int32, (256, 128), 0)
    coarse = lax.broadcasted_iota(jnp.int32, (256, 128), 1)
    return jnp.where((fine == 2 * coarse) | (fine == 2 * coarse + 1), 0.25, 0.0).astype(bf16)


def split_dot(value, matrix):
    high = value.astype(bf16)
    low = (value - high.astype(f32)).astype(bf16)
    return jnp.dot(high, matrix, preferred_element_type=f32) + jnp.dot(
        low, matrix, preferred_element_type=f32
    )


def forward_body(mask, u, u_lo, u_hi, lam, matrix, bias, diag, cot, sens, state, start, factor, wide0, wide1, turn):
    for z in range(8):
        source, place = ((u_lo, z), (u, z - 2), (u_hi, z - 6))[(z >= 2) + (z >= 6)]
        to_rows(source, place, turn)
        for pair in range(4):
            value = pair_of(turn, pair).astype(bf16)
            put(wide0, z, 0, pair, value)
            if 1 <= z <= 6:
                start[z - 1, :, pair * 256 : pair * 256 + 256] = value
    offset = bias[...]

    def first(z, carry):
        parts = products(matrix, wide0, z)
        for pair in range(4):
            cols = slice(pair * 256, pair * 256 + 256)
            tanh = jnp.tanh(combined(parts, pair) + offset)
            sens[z, :, cols] = 1.0 - tanh * tanh
            value = (start[z, :, cols].astype(f32) + STEP * tanh) * mask[z]
            value = value.astype(bf16)
            state[z, :, cols] = value
            put(wide1, z, 0, pair, value)
        return carry

    lax.fori_loop(0, 6, first, 0)
    average = averaging()

    def second(z, carry):
        parts = products(matrix, wide1, z)
        to_rows(lam, z, turn)
        for pair in range(4):
            cols = slice(pair * 256, pair * 256 + 256)
            tanh = jnp.tanh(combined(parts, pair) + offset)
            cot[z, :, cols] = ((1.0 - tanh * tanh) * pair_of(turn, pair)).astype(bf16)
            both = sens[z + 1, 0:64, cols] + sens[z + 1, 64:128, cols]
            coarse = jnp.dot(both.astype(bf16), average, preferred_element_type=f32)
            factor[z, pair] = (coarse * diag[...]).astype(bf16)
        return carry

    lax.fori_loop(0, 4, second, 0)


def forward(mask, u, u_lo, u_hi, lam, matrix, bias, diag):
    vmem = pl.BlockSpec(memory_space=pltpu.VMEM)
    return pl.pallas_call(
        forward_body,
        out_shape=(
            jax.ShapeDtypeStruct((4, 128, 1024), bf16),
            jax.ShapeDtypeStruct((6, 128, 1024), f32),
            jax.ShapeDtypeStruct((6, 128, 1024), bf16),
            jax.ShapeDtypeStruct((6, 128, 1024), bf16),
            jax.ShapeDtypeStruct((4, 4, 64, 128), bf16),
        ),
        in_specs=[pl.BlockSpec(memory_space=pltpu.SMEM)] + [vmem] * 7,
        scratch_shapes=[
            pltpu.VMEM((8 * 384, 1024), bf16),
            pltpu.VMEM((6 * 384, 1024), bf16),
            pltpu.VMEM((2, 512, 128), f32),
        ],
        compiler_params=PARAMS,
        name="forward",
    )(mask, u, u_lo, u_hi, lam, matrix, bias, diag)


def backward_body(mask, cot1, cot_lo, cot_hi, lam, lam_lo, lam_hi, sens, matrix, factor, cot0, coarse, average_lam, wide1, wide0, middle, turn):
    for z in range(8):
        source, place = ((cot_lo, z), (cot1, z - 2), (cot_hi, z - 6))[(z >= 2) + (z >= 6)]
        for pair in range(4):
            put(wide1, z, 0, pair, source[place, :, pair * 256 : pair * 256 + 256])

    def first(z, source, place):
        parts = products(matrix, wide1, z)
        to_rows(source, place, turn)
        for pair in range(4):
            cols = slice(pair * 256, pair * 256 + 256)
            value = pair_of(turn, pair) + STEP * combined(parts, pair)
            middle[z, :, cols] = value
            value = (sens[z, :, cols] * value * mask[z]).astype(bf16)
            put(wide0, z, 0, pair, value)
            if source is lam:
                cot0[place, :, cols] = value

    def inner(z, carry):
        first(z + 1, lam, z)
        return carry

    first(0, lam_lo, 0)
    lax.fori_loop(0, 4, inner, 0)
    first(5, lam_hi, 0)
    average = averaging()

    def second(z, carry):
        parts = products(matrix, wide0, z)
        to_rows(lam, z, turn)
        for pair in range(4):
            cols = slice(pair * 256, pair * 256 + 256)
            value = middle[z + 1, :, cols] + STEP * combined(parts, pair)
            back = split_dot(value[0:64] + value[64:128], average)
            here = split_dot(row_of(turn, 2 * pair) + row_of(turn, 2 * pair + 1), average)
            average_lam[z, pair] = here
            coarse[z, pair] = (back - here - factor[z, pair].astype(f32) * here).astype(bf16)
        return carry

    lax.fori_loop(0, 4, second, 0)


def backward(mask, cot1, cot_lo, cot_hi, lam, lam_lo, lam_hi, sens, matrix, factor):
    vmem = pl.BlockSpec(memory_space=pltpu.VMEM)
    return pl.pallas_call(
        backward_body,
        out_shape=(
            jax.ShapeDtypeStruct((4, 128, 1024), bf16),
            jax.ShapeDtypeStruct((4, 4, 64, 128), bf16),
            jax.ShapeDtypeStruct((4, 4, 64, 128), f32),
        ),
        in_specs=[pl.BlockSpec(memory_space=pltpu.SMEM)] + [vmem] * 9,
        scratch_shapes=[
            pltpu.VMEM((8 * 384, 1024), bf16),
            pltpu.VMEM((6 * 384, 1024), bf16),
            pltpu.VMEM((6, 128, 1024), f32),
            pltpu.VMEM((2, 512, 128), f32),
        ],
        compiler_params=PARAMS,
        name="backward",
    )(mask, cot1, cot_lo, cot_hi, lam, lam_lo, lam_hi, sens, matrix, factor)


def gradient_body(scale, cot, state, *refs):
    earlier = refs[0] if len(refs) == 5 else None
    out, wide, widened_cot, total = refs[-4:]
    for z in range(6):
        for pair in range(4):
            put(wide, z, 0, pair, state[z, :, pair * 256 : pair * 256 + 256])
    sums = jnp.zeros((128, 128), f32)
    zero = jnp.zeros((64, 256), bf16)
    for z in range(4):
        value = cot[z]
        widened_cot[z, 0:128] = value
        widened_cot[z, 128:192] = jnp.concatenate([zero, value[64:128, :768]], 1)
        widened_cot[z, 192:256] = jnp.concatenate([value[0:64, 256:], zero], 1)
        for part in range(8):
            sums = sums + value[:, part * 128 : part * 128 + 128].astype(f32)
    total[...] = jnp.zeros_like(total)

    def plane(z, carry):
        base = pl.multiple_of(z * 384, 384)
        total[...] += lax.dot_general(
            widened_cot[z],
            wide[pl.ds(base, 1152), :],
            (((1,), (1,)), ((), ())),
            preferred_element_type=f32,
        )
        return carry

    lax.fori_loop(0, 4, plane, 0)
    lower = lax.broadcasted_iota(jnp.int32, (64, 128), 1) < 64

    def give(block, value):
        value = value * scale
        out[block] = value if earlier is None else value + earlier[block]

    for tap in range(9):
        cols = slice(tap * 128, tap * 128 + 128)
        rows = [total[64 * q : 64 * q + 64, cols] for q in range(4)]
        taps = [jnp.where(lower, rows[1], rows[3]), jnp.where(lower, rows[0], rows[1]), jnp.where(lower, rows[2], rows[0])]
        taps = [value + pltpu.roll(value, 64, 1) for value in taps]
        give(tap, jnp.where(lower, taps[0], taps[1]))
        if tap % 2 == 0:
            kept = taps[2]
        else:
            give(9 + tap // 2, jnp.where(lower, kept, taps[2]))
    give(13, kept)
    give(14, sums[0:64] + sums[64:128])
    give(15, jnp.zeros((64, 128), f32))


def gradient(scale, cot, state, earlier=None):
    return pl.pallas_call(
        functools.partial(gradient_body, scale),
        out_shape=jax.ShapeDtypeStruct((16, 64, 128), f32),
        scratch_shapes=[
            pltpu.VMEM((6 * 384, 1024), bf16),
            pltpu.VMEM((4, 256, 1024), bf16),
            pltpu.VMEM((256, 1152), f32),
        ],
        compiler_params=PARAMS,
        name="gradient",
    )(*((cot, state) if earlier is None else (cot, state, earlier)))


def taps_body(summed, out):
    for a in range(3):
        for c in range(3):
            tap = 3 * a + c
            out[9 * a + c] = summed[tap][:, :64]
            out[9 * a + 3 + c] = summed[tap][:, 64:]
            half = 64 * (tap % 2)
            out[9 * a + 6 + c] = summed[9 + tap // 2][:, half : half + 64]


def taps_of(summed):
    return pl.pallas_call(
        taps_body,
        out_shape=jax.ShapeDtypeStruct((27, 64, 64), f32),
        compiler_params=PARAMS,
        name="taps",
    )(summed)


def sweep_body(factor, coarse, out):
    value = jnp.zeros(coarse.shape[1:], f32)
    out[0] = value.astype(bf16)
    for group in range(coarse.shape[0] - 1):
        value = value + factor[group].astype(f32) * value + coarse[group].astype(f32)
        out[group + 1] = value.astype(bf16)


def sweep(factor, coarse):
    return pl.pallas_call(
        sweep_body,
        out_shape=jax.ShapeDtypeStruct(coarse.shape, bf16),
        compiler_params=PARAMS,
        name="sweep",
    )(factor, coarse)


def finish_body(lam, average_lam, carried, out, turn):
    fine = lax.broadcasted_iota(jnp.int32, (128, 256), 1)
    coarse = lax.broadcasted_iota(jnp.int32, (128, 256), 0)
    copies = jnp.where((fine == 2 * coarse) | (fine == 2 * coarse + 1), 1.0, 0.0).astype(bf16)

    def plane(z, carry):
        for pair in range(4):
            value = split_dot(carried[z, pair].astype(f32) - average_lam[z, pair], copies)
            for half in range(2):
                for x in (2 * pair, 2 * pair + 1):
                    turn[half, pl.ds(x, 64, stride=8), :] = value[:, half * 128 : half * 128 + 128]
        added = jnp.concatenate([turn[0], turn[1]], 1).reshape(64, 8, 256)
        out[:, z] = lam[:, z] + added
        return carry

    lax.fori_loop(0, 4, plane, 0)


def finish(lam, average_lam, carried):
    return pl.pallas_call(
        finish_body,
        out_shape=jax.ShapeDtypeStruct((64, 4, 8, 256), f32),
        scratch_shapes=[pltpu.VMEM((2, 512, 128), f32)],
        compiler_params=PARAMS,
        name="finish",
    )(lam, average_lam, carried)


def tap_matrix(weight):
    taps = weight.reshape(3, 3, 3, 64, 64).transpose(1, 3, 0, 2, 4)
    none = jnp.zeros_like(taps[0])
    even = jnp.stack([taps[1], taps[0], taps[2], none])
    odd = jnp.stack([taps[2], taps[1], none, taps[0]])
    return jnp.stack([even, odd], 4).reshape(256, 1152)


def neighbours(low_part, high_part):
    count = lax.axis_size("slab")
    up = [(i, i + 1) for i in range(count - 1)]
    down = [(i + 1, i) for i in range(count - 1)]
    return lax.ppermute(high_part, "slab", up), lax.ppermute(low_part, "slab", down)


def exchanged(value, axes):
    return lax.all_to_all(value, axes, 0, 0, tiled=True)


def on_device(u_states, lam_points, weight, bias):
    u, lam = u_states[0], lam_points[0]
    slab, slabs = lax.axis_index("slab"), lax.axis_size("slab")
    devices = slabs * lax.axis_size("tm")
    u_lo, u_hi = neighbours(u[:, :2], u[:, 2:])
    lam_lo, lam_hi = neighbours(lam[:, :1].astype(bf16), lam[:, 3:].astype(bf16))
    matrix = tap_matrix(weight)
    flipped = tap_matrix(weight[::-1].transpose(0, 2, 1))
    offset = jnp.broadcast_to(jnp.tile(bias, 2)[:, None], (128, 256))
    diagonal = jnp.diagonal(weight[13]).astype(f32)
    diag = jnp.broadcast_to((2.0 * STEP * diagonal)[:, None], (64, 128))
    ones = jnp.ones((4,), f32)
    mask = jnp.concatenate([(slab > 0).astype(f32)[None], ones, (slab < slabs - 1).astype(f32)[None]])
    cot1, sens, state, start, factor = forward(mask, u, u_lo, u_hi, lam, matrix, offset, diag)
    cot_lo, cot_hi = neighbours(cot1[:2], cot1[2:])
    factors = exchanged(factor.reshape(8, 2, 64, 128), "tm")
    scale = STEP / math.sqrt(2 * devices * 4 * 8 * 256)
    partial_sum = gradient(scale, cot1, state)
    cot0, coarse, average_lam = backward(mask, cot1, cot_lo, cot_hi, lam, lam_lo, lam_hi, sens, flipped, factor)
    pieces = exchanged(coarse.reshape(8, 2, 64, 128), "tm")
    total = gradient(scale, cot0, start, partial_sum)
    parts = exchanged(total.reshape(devices, 8, 128), ("tm", "slab"))
    carried = exchanged(sweep(factors, pieces), "tm").reshape(4, 4, 64, 128)
    mine = jnp.sum(parts, axis=0)
    summed = exchanged(jnp.broadcast_to(mine[None], parts.shape), ("tm", "slab")).reshape(16, 64, 128)
    updated = finish(lam, average_lam, carried)
    return updated[None], taps_of(summed), jnp.sum(summed[14], axis=1)


def solution(mesh):
    in_specs = (P("tm", None, "slab", None, None), P("tm", None, "slab", None, None), P(), P())
    out_specs = (P("tm", None, "slab", None, None), P(), P())
    return jax.shard_map(
        on_device, mesh=mesh, in_specs=in_specs, out_specs=out_specs, check_vma=False
    )
```

time: 785 us -> 162 us (0.21)
  the two profiles are of different devices: /device:TPU:24 before, /device:TPU:1 now
where the time goes in v1:
time: 162 us; the launch traced here: 161 us
  Pallas kernels  55.7 us (34%)
  starting transfers between devices  52.8 us (33%)
  waiting for transfers between devices  31.8 us (20%)
  local copies, waits for them, and re-layouts  17 us (10%)
  other arithmetic  2.63 us (2%)
    all_to_all x5, starting transfers between devices, exchanged(): return lax.all_to_all(value, axes, 0, 0, tiled=True)  36.3 us
    all_to_all x5, waiting for transfers between devices, exchanged(): return lax.all_to_all(value, axes, 0, 0, tiled=True)  28.5 us
    pallas_call x1, Pallas kernels, forward(): pl.pallas_call(forward_body, out_shape=(jax.ShapeDtypeStruct((4, 128, 102...  16.1 us
    pallas_call x1, Pallas kernels, backward(): pl.pallas_call(backward_body, out_shape=(jax.ShapeDtypeStruct((4, 128, 10...  16 us
    pallas_call x2, Pallas kernels, gradient(): pl.pallas_call(functools.partial(gradient_body, scale), out_shape=jax.Sha...  15.3 us
    ppermute x3, starting transfers between devices, neighbours(): lax.ppermute(high_part, 'slab', up)  10.2 us
    ppermute x3, starting transfers between devices, neighbours(): lax.ppermute(low_part, 'slab', down)  6.28 us
    pallas_call x1, Pallas kernels, finish(): pl.pallas_call(finish_body, out_shape=jax.ShapeDtypeStruct((64, 4, 8, 256...  4.37 us
  transfers between devices with their start and end apart: 11, of which 4 were waited for; matrix products, arithmetic and copies ran while one was open for 6% of the time, Pallas kernels for 23%

profile of v1, /device:TPU:1, one launch (start us, length us, event | category | flops | bytes accessed | tf_op | source)
XLA Modules:
  0.0 160.8 jit_solution(7780959044040296422)
XLA Ops:
  0.6 2.3 %fusion.8 = (bf16[64,2,8,256]{3,2,1,0:T(8,128)(2,1)}, bf16[64,2,8,256]{3,2,1,0:T(8,128)(2,1)}) fusion(bf16[64,4,8,256]{3,2,1,0:T(8,128)(2,1)} %bitcast.34), kind=kLoop, calls=%fused_computation.21 | loop fusion | bytes 2097152 | tf_op jit(solution)/shard_map/slice | solution.py:360
  3.0 4.9 %collective-permute-start = (bf16[64,2,8,256]{3,2,1,0:T(8,128)(2,1)}, bf16[64,2,8,256]{3,2,1,0:T(8,128)(2,1)S(1)}, u32[]{:S(2)}, u32[]{:S(2)}) collective-permute-start(bf16[64,2,8,256]{3,2,1,0:T(8,128)(2,1)} %get-tuple-element.24), channel_id=1, source_target_pairs={{0,1},{1,2},{2,3},{3,4},{4,5},{5,6},{6,7},{7,8},{8,9},{9,10},{10,1... | collective-permute-start | bytes 1572872 | tf_op jit(solution)/shard_map/ppermute | solution.py:349
  7.9 1.9 %collective-permute-start.1 = (bf16[64,2,8,256]{3,2,1,0:T(8,128)(2,1)}, bf16[64,2,8,256]{3,2,1,0:T(8,128)(2,1)}, u32[]{:S(2)}, u32[]{:S(2)}) collective-permute-start(bf16[64,2,8,256]{3,2,1,0:T(8,128)(2,1)} %get-tuple-element.23), channel_id=1, source_target_pairs={{1,0},{2,1},{3,2},{4,3},{5,4},{6,5},{7,6},{8,7},{9,8},{10,9},{11,1... | collective-permute-start | bytes 1572872 | tf_op jit(solution)/shard_map/ppermute | solution.py:349
  9.8 0.2 copy.14
  10.2 0.3 fusion.5
  10.6 0.5 pad_maximum_fusion
  11.1 1.2 copy.13
  12.3 0.0 copy-start.9
  12.3 1.5 reshape.44.matrix
  13.8 0.1 broadcast_in_dim.42
  13.9 0.9 gather_fusion
  14.8 0.7 pad_maximum_fusion.6.mask
  15.5 3.2 %collective-permute-done.1.u_hi = bf16[64,2,8,256]{3,2,1,0:T(8,128)(2,1)} collective-permute-done((bf16[64,2,8,256]{3,2,1,0:T(8,128)(2,1)}, bf16[64,2,8,256]{3,2,1,0:T(8,128)(2,1)}, u32[]{:S(2)}, u32[]{:S(2)}) %collective-permute-start.1) | collective-permute-done | bytes 524320 | tf_op jit(solution)/shard_map/ppermute | solution.py:349
  18.7 0.7 broadcast_in_dim.43.bias
  19.4 0.7 broadcast_in_dim.44.diag
  20.1 16.1 %forward.1 = (bf16[4,128,1024]{2,1,0:T(8,128)(2,1)}, f32[6,128,1024]{2,1,0:T(8,128)}, bf16[6,128,1024]{2,1,0:T(8,128)(2,1)}, bf16[6,128,1024]{2,1,0:T(8,128)(2,1)}, bf16[4,4,64,128]{3,2,1,0:T(8,128)(2,1)}) custom-call(f32[6]{0:T(128)} %pad_maximum_fusion.6.mask, bf16[64,4,8,256]{3,2,1,0:T(8,128)(2,1)} %bitcast.35, bf16[64,2,8,256]{3,2,1,0:T(8,128)(2,1)} %copy-done.6, ...), custom_call_target="tpu_custom_call" | custom-call | tf_op jit(solution)/shard_map/forward/pallas_call | solution.py:127
  36.2 2.4 %fusion.7 = (bf16[2,128,1024]{2,1,0:T(8,128)(2,1)}, bf16[2,128,1024]{2,1,0:T(8,128)(2,1)}) fusion(bf16[4,128,1024]{2,1,0:T(8,128)(2,1)} %get-tuple-element.11.cot1.cot), kind=kLoop, calls=%fused_computation.20 | loop fusion | bytes 2097152 | tf_op jit(solution)/shard_map/slice | solution.py:370
  38.6 1.9 %collective-permute-start.2 = (bf16[2,128,1024]{2,1,0:T(8,128)(2,1)}, bf16[2,128,1024]{2,1,0:T(8,128)(2,1)S(1)}, u32[]{:S(2)}, u32[]{:S(2)}) collective-permute-start(bf16[2,128,1024]{2,1,0:T(8,128)(2,1)} %get-tuple-element.22), channel_id=1, source_target_pairs={{0,1},{1,2},{2,3},{3,4},{4,5},{5,6},{6,7},{7,8},{8,9},{9,10},{10,1... | collective-permute-start | bytes 1572872 | tf_op jit(solution)/shard_map/ppermute | solution.py:349
  40.6 2.4 %collective-permute-start.3 = (bf16[2,128,1024]{2,1,0:T(8,128)(2,1)}, bf16[2,128,1024]{2,1,0:T(8,128)(2,1)}, u32[]{:S(2)}, u32[]{:S(2)}) collective-permute-start(bf16[2,128,1024]{2,1,0:T(8,128)(2,1)} %get-tuple-element.21), channel_id=1, source_target_pairs={{1,0},{2,1},{3,2},{4,3},{5,4},{6,5},{7,6},{8,7},{9,8},{10,9},{11,1... | collective-permute-start | bytes 1572872 | tf_op jit(solution)/shard_map/ppermute | solution.py:349
  43.0 0.2 bitcast_convert_fusion
  43.2 0.8 fusion.6
  44.0 3.4 %collective-permute-start.4 = (bf16[64,1,8,256]{3,2,1,0:T(8,128)(2,1)}, bf16[64,1,8,256]{3,2,1,0:T(8,128)(2,1)S(1)}, u32[]{:S(2)}, u32[]{:S(2)}) collective-permute-start(bf16[64,1,8,256]{3,2,1,0:T(8,128)(2,1)} %get-tuple-element.20), channel_id=1, source_target_pairs={{0,1},{1,2},{2,3},{3,4},{4,5},{5,6},{6,7},{7,8},{8,9},{9,10},{10,1... | collective-permute-start | bytes 786440 | tf_op jit(solution)/shard_map/ppermute | solution.py:349
  47.4 1.9 %collective-permute-start.5 = (bf16[64,1,8,256]{3,2,1,0:T(8,128)(2,1)}, bf16[64,1,8,256]{3,2,1,0:T(8,128)(2,1)}, u32[]{:S(2)}, u32[]{:S(2)}) collective-permute-start(bf16[64,1,8,256]{3,2,1,0:T(8,128)(2,1)} %get-tuple-element.19), channel_id=1, source_target_pairs={{1,0},{2,1},{3,2},{4,3},{5,4},{6,5},{7,6},{8,7},{9,8},{10,9},{11,1... | collective-permute-start | bytes 786440 | tf_op jit(solution)/shard_map/ppermute | solution.py:349
  49.4 5.0 %all-to-all-start = ((bf16[8,2,64,128]{3,2,1,0:T(8,128)(2,1)}), bf16[8,2,64,128]{3,2,1,0:T(8,128)(2,1)S(1)}, u32[]{:S(2)}, u32[]{:S(2)}) async-start(bf16[8,2,64,128]{3,2,1,0:T(8,128)(2,1)} %bitcast.18), calls=%async_computation | async-start | bytes 524288 | tf_op jit(solution)/shard_map/all_to_all | solution.py:353
  54.4 1.2 copy.17
  55.6 1.5 reshape.46.matrix
  57.1 0.0 collective-permute-done.4.lam_lo
  57.1 0.0 collective-permute-done.5.lam_hi
  57.2 0.7 copy-done.8
  57.8 0.2 copy-done.7
  58.1 16.0 %backward.1 = (bf16[4,128,1024]{2,1,0:T(8,128)(2,1)}, bf16[4,4,64,128]{3,2,1,0:T(8,128)(2,1)}, f32[4,4,64,128]{3,2,1,0:T(8,128)}) custom-call(f32[6]{0:T(128)} %pad_maximum_fusion.6.mask, bf16[4,128,1024]{2,1,0:T(8,128)(2,1)} %get-tuple-element.11.cot1.cot, bf16[2,128,1024]{2,1,0:T(8,128)(2,1)} %copy-done.7, ...), custom_call_target="tpu_custom_call" | custom-call | tf_op jit(solution)/shard_map/backward/pallas_call | solution.py:191
  74.1 5.2 %all-to-all-start.1 = ((bf16[8,2,64,128]{3,2,1,0:T(8,128)(2,1)}), bf16[8,2,64,128]{3,2,1,0:T(8,128)(2,1)S(1)}, u32[]{:S(2)}, u32[]{:S(2)}) async-start(bf16[8,2,64,128]{3,2,1,0:T(8,128)(2,1)} %bitcast.42), calls=%async_computation.1 | async-start | bytes 524288 | tf_op jit(solution)/shard_map/all_to_all | solution.py:353
  79.3 7.6 %gradient.2.refs_0_ = f32[16,64,128]{2,1,0:T(8,128)} custom-call(bf16[4,128,1024]{2,1,0:T(8,128)(2,1)} %get-tuple-element.11.cot1.cot, bf16[6,128,1024]{2,1,0:T(8,128)(2,1)} %get-tuple-element.18.state), custom_call_target="tpu_custom_call" | custom-call | tf_op jit(solution)/shard_map/gradient/pallas_call | solution.py:260
  86.9 7.7 %gradient.3 = f32[16,64,128]{2,1,0:T(8,128)} custom-call(bf16[4,128,1024]{2,1,0:T(8,128)(2,1)} %get-tuple-element.16.cot, bf16[6,128,1024]{2,1,0:T(8,128)(2,1)} %get-tuple-element.17.state, f32[16,64,128]{2,1,0:T(8,128)} %gradient.2.refs_0_), custom_call_target="tpu_custom_call" | custom-call | tf_op jit(solution)/shard_map/gradient/pallas_call | solution.py:260
  94.6 18.3 %all-to-all-start.3 = ((f32[128,8,128]{2,1,0:T(8,128)}), f32[128,8,128]{2,1,0:T(8,128)S(1)}, u32[]{:S(2)}, u32[]{:S(2)}) async-start(f32[128,8,128]{2,1,0:T(8,128)} %bitcast.37), calls=%async_computation.3 | async-start | bytes 1048576 | tf_op jit(solution)/shard_map/all_to_all | solution.py:353
  112.9 1.8 %sweep.1 = bf16[8,2,64,128]{3,2,1,0:T(8,128)(2,1)} custom-call(bf16[8,2,64,128]{3,2,1,0:T(8,128)(2,1)} %copy-done.3, bf16[8,2,64,128]{3,2,1,0:T(8,128)(2,1)} %copy-done.4), custom_call_target="tpu_custom_call" | custom-call | tf_op jit(solution)/shard_map/sweep/pallas_call | solution.py:301
  114.7 11.9 %all-to-all-done.3 = f32[128,8,128]{2,1,0:T(8,128)S(1)} async-done(((f32[128,8,128]{2,1,0:T(8,128)}), f32[128,8,128]{2,1,0:T(8,128)S(1)}, u32[]{:S(2)}, u32[]{:S(2)}) %all-to-all-start.3) | async-done | bytes 524320 | tf_op jit(solution)/shard_map/all_to_all | solution.py:353
  126.7 3.4 %all-to-all-start.2 = ((bf16[8,2,64,128]{3,2,1,0:T(8,128)(2,1)}), bf16[8,2,64,128]{3,2,1,0:T(8,128)(2,1)S(1)}, u32[]{:S(2)}, u32[]{:S(2)}) async-start(bf16[8,2,64,128]{3,2,1,0:T(8,128)(2,1)} %sweep.1), calls=%async_computation.2 | async-start | bytes 524288 | tf_op jit(solution)/shard_map/all_to_all | solution.py:353
  130.1 0.1 reduce_sum.20
  130.2 7.2 %all-to-all-done.2 = bf16[8,2,64,128]{3,2,1,0:T(8,128)(2,1)S(1)} async-done(((bf16[8,2,64,128]{3,2,1,0:T(8,128)(2,1)}), bf16[8,2,64,128]{3,2,1,0:T(8,128)(2,1)S(1)}, u32[]{:S(2)}, u32[]{:S(2)}) %all-to-all-start.2) | async-done | bytes 262176 | tf_op jit(solution)/shard_map/all_to_all | solution.py:353
  137.4 0.9 broadcast_in_dim.46
  138.3 4.3 %all-to-all-start.4 = ((f32[128,8,128]{2,1,0:T(8,128)}), f32[128,8,128]{2,1,0:T(8,128)S(1)}, u32[]{:S(2)}, u32[]{:S(2)}) async-start(f32[128,8,128]{2,1,0:T(8,128)} %broadcast_in_dim.46), calls=%async_computation.4 | async-start | bytes 1048576 | tf_op jit(solution)/shard_map/all_to_all | solution.py:353
  142.7 4.4 %finish.1 = f32[64,4,8,256]{3,2,1,0:T(8,128)} custom-call(f32[64,4,8,256]{3,2,1,0:T(8,128)} %bitcast.33, f32[4,4,64,128]{3,2,1,0:T(8,128)} %get-tuple-element.14.average_lam, bf16[4,4,64,128]{3,2,1,0:T(8,128)(2,1)} %bitcast.41), custom_call_target="tpu_custom_call" | custom-call | tf_op jit(solution)/shard_map/finish/pallas_call | solution.py:328
  147.0 9.4 %all-to-all-done.4 = f32[128,8,128]{2,1,0:T(8,128)S(1)} async-done(((f32[128,8,128]{2,1,0:T(8,128)}), f32[128,8,128]{2,1,0:T(8,128)S(1)}, u32[]{:S(2)}, u32[]{:S(2)}) %all-to-all-start.4) | async-done | bytes 524320 | tf_op jit(solution)/shard_map/all_to_all | solution.py:353
  156.4 0.8 copy-done.1
  157.2 2.1 %taps.1 = f32[27,64,64]{2,1,0:T(8,128)} custom-call(f32[16,64,128]{2,1,0:T(8,128)} %bitcast.36), custom_call_target="tpu_custom_call" | custom-call | tf_op jit(solution)/shard_map/taps/pallas_call | solution.py:284
  159.3 0.8 slice_reduce_fusion
  160.2 0.6 reduce_sum.22
  (30 shorter events, 0.2 us)
Async XLA Ops:
  0.6 9.2 %copy-start.2 = (bf16[27,64,64]{2,1,0:T(8,128)(2,1)S(1)}, bf16[27,64,64]{2,1,0:T(8,128)(2,1)}, u32[]{:S(2)}) copy-start(bf16[27,64,64]{2,1,0:T(8,128)(2,1)} %param.6) | copy-start | bytes 663556
  3.0 12.5 %collective-permute-start = (bf16[64,2,8,256]{3,2,1,0:T(8,128)(2,1)}, bf16[64,2,8,256]{3,2,1,0:T(8,128)(2,1)S(1)}, u32[]{:S(2)}, u32[]{:S(2)}) collective-permute-start(bf16[64,2,8,256]{3,2,1,0:T(8,128)(2,1)} %get-tuple-element.24), channel_id=1, source_target_pairs={{0,1},{1,2},{2,3},{3,4},{4,5},{5,6},{6,7},{7,8},{8,9},{9,10},{10,1... | collective-permute-start | bytes 1572872 | tf_op jit(solution)/shard_map/ppermute | solution.py:349
  7.9 10.8 %collective-permute-start.1 = (bf16[64,2,8,256]{3,2,1,0:T(8,128)(2,1)}, bf16[64,2,8,256]{3,2,1,0:T(8,128)(2,1)}, u32[]{:S(2)}, u32[]{:S(2)}) collective-permute-start(bf16[64,2,8,256]{3,2,1,0:T(8,128)(2,1)} %get-tuple-element.23), channel_id=1, source_target_pairs={{1,0},{2,1},{3,2},{4,3},{5,4},{6,5},{7,6},{8,7},{9,8},{10,9},{11,1... | collective-permute-start | bytes 1572872 | tf_op jit(solution)/shard_map/ppermute | solution.py:349
  12.3 1.5 copy-start.9
  15.5 4.7 %copy-start.6 = (bf16[64,2,8,256]{3,2,1,0:T(8,128)(2,1)}, bf16[64,2,8,256]{3,2,1,0:T(8,128)(2,1)S(1)}, u32[]{:S(2)}) copy-start(bf16[64,2,8,256]{3,2,1,0:T(8,128)(2,1)S(1)} %collective-permute-done.u_lo) | copy-start | bytes 1572868
  36.2 6.8 %copy-start = (f32[1,64,4,8,256]{4,3,2,1,0:T(8,128)S(1)}, f32[1,64,4,8,256]{4,3,2,1,0:T(8,128)}, u32[]{:S(2)}) copy-start(f32[1,64,4,8,256]{4,3,2,1,0:T(8,128)} %param.5) | copy-start | bytes 6291460
  38.6 18.5 %collective-permute-start.2 = (bf16[2,128,1024]{2,1,0:T(8,128)(2,1)}, bf16[2,128,1024]{2,1,0:T(8,128)(2,1)S(1)}, u32[]{:S(2)}, u32[]{:S(2)}) collective-permute-start(bf16[2,128,1024]{2,1,0:T(8,128)(2,1)} %get-tuple-element.22), channel_id=1, source_target_pairs={{0,1},{1,2},{2,3},{3,4},{4,5},{5,6},{6,7},{7,8},{8,9},{9,10},{10,1... | collective-permute-start | bytes 1572872 | tf_op jit(solution)/shard_map/ppermute | solution.py:349
  40.6 16.6 %collective-permute-start.3 = (bf16[2,128,1024]{2,1,0:T(8,128)(2,1)}, bf16[2,128,1024]{2,1,0:T(8,128)(2,1)}, u32[]{:S(2)}, u32[]{:S(2)}) collective-permute-start(bf16[2,128,1024]{2,1,0:T(8,128)(2,1)} %get-tuple-element.21), channel_id=1, source_target_pairs={{1,0},{2,1},{3,2},{4,3},{5,4},{6,5},{7,6},{8,7},{9,8},{10,9},{11,1... | collective-permute-start | bytes 1572872 | tf_op jit(solution)/shard_map/ppermute | solution.py:349
  44.0 13.1 %collective-permute-start.4 = (bf16[64,1,8,256]{3,2,1,0:T(8,128)(2,1)}, bf16[64,1,8,256]{3,2,1,0:T(8,128)(2,1)S(1)}, u32[]{:S(2)}, u32[]{:S(2)}) collective-permute-start(bf16[64,1,8,256]{3,2,1,0:T(8,128)(2,1)} %get-tuple-element.20), channel_id=1, source_target_pairs={{0,1},{1,2},{2,3},{3,4},{4,5},{5,6},{6,7},{7,8},{8,9},{9,10},{10,1... | collective-permute-start | bytes 786440 | tf_op jit(solution)/shard_map/ppermute | solution.py:349
  47.4 9.7 %collective-permute-start.5 = (bf16[64,1,8,256]{3,2,1,0:T(8,128)(2,1)}, bf16[64,1,8,256]{3,2,1,0:T(8,128)(2,1)}, u32[]{:S(2)}, u32[]{:S(2)}) collective-permute-start(bf16[64,1,8,256]{3,2,1,0:T(8,128)(2,1)} %get-tuple-element.19), channel_id=1, source_target_pairs={{1,0},{2,1},{3,2},{4,3},{5,4},{6,5},{7,6},{8,7},{9,8},{10,9},{11,1... | collective-permute-start | bytes 786440 | tf_op jit(solution)/shard_map/ppermute | solution.py:349
  49.4 24.8 %all-to-all-start = ((bf16[8,2,64,128]{3,2,1,0:T(8,128)(2,1)}), bf16[8,2,64,128]{3,2,1,0:T(8,128)(2,1)S(1)}, u32[]{:S(2)}, u32[]{:S(2)}) async-start(bf16[8,2,64,128]{3,2,1,0:T(8,128)(2,1)} %bitcast.18), calls=%async_computation | async-start | bytes 524288 | tf_op jit(solution)/shard_map/all_to_all | solution.py:353
  57.1 0.7 copy-start.8
  57.1 0.9 copy-start.7
  74.1 12.8 %copy-start.3 = (bf16[8,2,64,128]{3,2,1,0:T(8,128)(2,1)}, bf16[8,2,64,128]{3,2,1,0:T(8,128)(2,1)S(1)}, u32[]{:S(2)}) copy-start(bf16[8,2,64,128]{3,2,1,0:T(8,128)(2,1)S(1)} %all-to-all-done.factor) | copy-start | bytes 786436
  74.1 20.4 %all-to-all-start.1 = ((bf16[8,2,64,128]{3,2,1,0:T(8,128)(2,1)}), bf16[8,2,64,128]{3,2,1,0:T(8,128)(2,1)S(1)}, u32[]{:S(2)}, u32[]{:S(2)}) async-start(bf16[8,2,64,128]{3,2,1,0:T(8,128)(2,1)} %bitcast.42), calls=%async_computation.1 | async-start | bytes 524288 | tf_op jit(solution)/shard_map/all_to_all | solution.py:353
  94.6 18.4 %copy-start.4 = (bf16[8,2,64,128]{3,2,1,0:T(8,128)(2,1)}, bf16[8,2,64,128]{3,2,1,0:T(8,128)(2,1)S(1)}, u32[]{:S(2)}) copy-start(bf16[8,2,64,128]{3,2,1,0:T(8,128)(2,1)S(1)} %all-to-all-done.1.coarse) | copy-start | bytes 786436
  94.6 32.1 %all-to-all-start.3 = ((f32[128,8,128]{2,1,0:T(8,128)}), f32[128,8,128]{2,1,0:T(8,128)S(1)}, u32[]{:S(2)}, u32[]{:S(2)}) async-start(f32[128,8,128]{2,1,0:T(8,128)} %bitcast.37), calls=%async_computation.3 | async-start | bytes 1048576 | tf_op jit(solution)/shard_map/all_to_all | solution.py:353
  126.7 10.8 %all-to-all-start.2 = ((bf16[8,2,64,128]{3,2,1,0:T(8,128)(2,1)}), bf16[8,2,64,128]{3,2,1,0:T(8,128)(2,1)S(1)}, u32[]{:S(2)}, u32[]{:S(2)}) async-start(bf16[8,2,64,128]{3,2,1,0:T(8,128)(2,1)} %sweep.1), calls=%async_computation.2 | async-start | bytes 524288 | tf_op jit(solution)/shard_map/all_to_all | solution.py:353
  137.4 5.2 %copy-start.5 = (bf16[8,2,64,128]{3,2,1,0:T(8,128)(2,1)}, bf16[8,2,64,128]{3,2,1,0:T(8,128)(2,1)S(1)}, u32[]{:S(2)}) copy-start(bf16[8,2,64,128]{3,2,1,0:T(8,128)(2,1)S(1)} %all-to-all-done.2) | copy-start | bytes 786436
  138.3 18.1 %all-to-all-start.4 = ((f32[128,8,128]{2,1,0:T(8,128)}), f32[128,8,128]{2,1,0:T(8,128)S(1)}, u32[]{:S(2)}, u32[]{:S(2)}) async-start(f32[128,8,128]{2,1,0:T(8,128)} %broadcast_in_dim.46), calls=%async_computation.4 | async-start | bytes 1048576 | tf_op jit(solution)/shard_map/all_to_all | solution.py:353
  156.4 0.8 copy-start.1

commit v2 on v1

v2 whole, which is shorter than its diff:
```python
import functools
import math

import jax
import jax.numpy as jnp
from jax import lax
from jax.experimental import pallas as pl
from jax.experimental.pallas import tpu as pltpu
from jax.sharding import PartitionSpec as P

f32, bf16 = jnp.float32, jnp.bfloat16
STEP = 0.25


def shifts(value):
    lane = lax.broadcasted_iota(jnp.int32, value.shape, 1)
    zero = jnp.zeros((), value.dtype)
    left = jnp.where(lane == 0, zero, pltpu.roll(value, 1, 1))
    right = jnp.where(lane == 255, zero, pltpu.roll(value, 255, 1))
    return left, right


def put(wide, plane, row, pair, value):
    count = value.shape[0]
    left, right = shifts(value)
    base = plane * 384 + row
    cols = slice(pair * 256, pair * 256 + 256)
    wide[pl.ds(base, count), cols] = left
    wide[pl.ds(base + 128, count), cols] = value
    wide[pl.ds(base + 256, count), cols] = right


def to_rows(source, z, turn):
    value = source[:, z].astype(f32).reshape(512, 256)
    turn[0] = value[:, :128]
    turn[1] = value[:, 128:]


def row_of(turn, x):
    return jnp.concatenate([turn[half, pl.ds(x, 64, stride=8), :] for half in range(2)], 1)


def pair_of(turn, pair):
    return jnp.concatenate([row_of(turn, 2 * pair), row_of(turn, 2 * pair + 1)], 0)


def products(matrix, wide, z):
    base = pl.multiple_of(z * 384, 384)
    return [
        jnp.dot(
            matrix[...],
            wide[pl.ds(base, 1152), pair * 256 : pair * 256 + 256],
            preferred_element_type=f32,
        )
        for pair in range(4)
    ]


def combined(parts, pair):
    low, high = parts[pair][0:64], parts[pair][64:128]
    if pair > 0:
        low = low + parts[pair - 1][192:256]
    if pair < 3:
        high = high + parts[pair + 1][128:192]
    return jnp.concatenate([low, high], 0)


def averaging():
    fine = lax.broadcasted_iota(jnp.int32, (256, 128), 0)
    coarse = lax.broadcasted_iota(jnp.int32, (256, 128), 1)
    return jnp.where((fine == 2 * coarse) | (fine == 2 * coarse + 1), 0.25, 0.0).astype(bf16)


def split_dot(value, matrix):
    high = value.astype(bf16)
    low = (value - high.astype(f32)).astype(bf16)
    return jnp.dot(high, matrix, preferred_element_type=f32) + jnp.dot(
        low, matrix, preferred_element_type=f32
    )


def field(planes, dtype):
    return pltpu.VMEM((planes, 128, 1024), dtype)


def widened(planes):
    return pltpu.VMEM((planes * 384, 1024), bf16)


def near(value):
    return pltpu.with_memory_space_constraint(value, pltpu.VMEM)


def run(body, name, micros, outs, ins, scratch=(), aliases=None, scalars=0, limit=8):
    in_specs = [pl.BlockSpec(memory_space=pltpu.SMEM)] * scalars
    in_specs += [pl.BlockSpec(memory_space=pltpu.VMEM)] * (len(ins) - scalars)
    return pl.pallas_call(
        body,
        out_shape=outs,
        in_specs=in_specs,
        scratch_shapes=list(scratch),
        input_output_aliases=aliases or {},
        compiler_params=pltpu.CompilerParams(vmem_limit_bytes=limit * 2**20),
        cost_estimate=pl.CostEstimate(flops=int(micros * 1.1e9), bytes_accessed=0, transcendentals=0),
        name=name,
    )(*ins)


TURN = pltpu.VMEM((2, 512, 128), f32)


def open_body(u, low, high, turn):
    for z in range(4):
        to_rows(u, z, turn)
        target = low if z < 2 else high
        for pair in range(4):
            target[z % 2, :, pair * 256 : pair * 256 + 256] = pair_of(turn, pair).astype(bf16)


def step_state(z, matrix, offset, wide0, wide1, sens, weight):
    parts = products(matrix, wide0, z)
    base = pl.multiple_of((z + 1) * 384, 384)
    for pair in range(4):
        cols = slice(pair * 256, pair * 256 + 256)
        tanh = jnp.tanh(combined(parts, pair) + offset)
        sens[z, :, cols] = 1.0 - tanh * tanh
        value = wide0[pl.ds(base + 128, 128), cols].astype(f32) + STEP * tanh
        if weight is not None:
            value = value * weight
        put(wide1, z, 0, pair, value.astype(bf16))


def inner_body(low, high, lam, matrix, bias, wide0, wide1, sens, lam_rows, average_lam, turn):
    average = averaging()
    for z in range(4):
        source = low if z < 2 else high
        for pair in range(4):
            put(wide0, z + 2, 0, pair, source[z % 2, :, pair * 256 : pair * 256 + 256])
    offset = bias[...]

    def inside(z, carry):
        step_state(z, matrix, offset, wide0, wide1, sens, None)
        return carry

    lax.fori_loop(2, 4, inside, 0)
    for z in range(4):
        to_rows(lam, z, turn)
        for pair in range(4):
            cols = slice(pair * 256, pair * 256 + 256)
            value = pair_of(turn, pair)
            lam_rows[z, :, cols] = value
            average_lam[z, pair] = split_dot(value[0:64] + value[64:128], average)


def forward_body(mask, wide0_in, wide1_in, sens_in, u_lo, u_hi, lam, matrix, bias, diag, wide0, wide1, sens, cot_low, cot_high, factor):
    for z in range(2):
        for pair in range(4):
            cols = slice(pair * 256, pair * 256 + 256)
            put(wide0, z, 0, pair, u_lo[z, :, cols])
            put(wide0, z + 6, 0, pair, u_hi[z, :, cols])
    offset = bias[...]

    def outside(index, carry):
        z = index + 2 * (index // 2)
        step_state(z, matrix, offset, wide0, wide1, sens, mask[z])
        return carry

    lax.fori_loop(0, 4, outside, 0)
    average = averaging()

    def second(z, target, place):
        parts = products(matrix, wide1, z)
        for pair in range(4):
            cols = slice(pair * 256, pair * 256 + 256)
            tanh = jnp.tanh(combined(parts, pair) + offset)
            target[place, :, cols] = ((1.0 - tanh * tanh) * lam[z, :, cols]).astype(bf16)
            both = sens[z + 1, 0:64, cols] + sens[z + 1, 64:128, cols]
            coarse = jnp.dot(both.astype(bf16), average, preferred_element_type=f32)
            factor[z, pair] = (coarse * diag[...]).astype(bf16)

    def second_low(z, carry):
        second(z, cot_low, z)
        return carry

    def second_high(z, carry):
        second(z + 2, cot_high, z)
        return carry

    cot_low[2] = lam[0].astype(bf16)
    cot_high[2] = lam[3].astype(bf16)
    lax.fori_loop(0, 2, second_low, 0)
    lax.fori_loop(0, 2, second_high, 0)


def step_back(z, matrix, wide1, wide0, middle, sens, lam, weight):
    parts = products(matrix, wide1, z)
    for pair in range(4):
        cols = slice(pair * 256, pair * 256 + 256)
        value = lam(cols) + STEP * combined(parts, pair)
        middle[z, :, cols] = value
        value = sens[z, :, cols] * value
        if weight is not None:
            value = value * weight
        put(wide0, z, 0, pair, value.astype(bf16))


def back_inner_body(low, high, lam, sens, matrix, wide1, wide0, middle):
    for z in range(4):
        source = low if z < 2 else high
        for pair in range(4):
            put(wide1, z + 2, 0, pair, source[z % 2, :, pair * 256 : pair * 256 + 256])

    def inside(z, carry):
        step_back(z, matrix, wide1, wide0, middle, sens, lambda cols: lam[z - 1, :, cols], None)
        return carry

    lax.fori_loop(2, 4, inside, 0)


def back_outer_body(mask, wide1_in, wide0_in, middle_in, cot_lo, cot_hi, lam, sens, matrix, wide1, wide0, middle):
    for z in range(2):
        for pair in range(4):
            cols = slice(pair * 256, pair * 256 + 256)
            put(wide1, z, 0, pair, cot_lo[z, :, cols])
            put(wide1, z + 6, 0, pair, cot_hi[z, :, cols])

    def outside(index, carry):
        z = 1 + 3 * index
        step_back(z, matrix, wide1, wide0, middle, sens, lambda cols: lam[z - 1, :, cols], None)
        return carry

    step_back(0, matrix, wide1, wide0, middle, sens, lambda cols: cot_lo[2, :, cols].astype(f32), mask[0])
    lax.fori_loop(0, 2, outside, 0)
    step_back(5, matrix, wide1, wide0, middle, sens, lambda cols: cot_hi[2, :, cols].astype(f32), mask[5])


def back_last_body(wide0, middle, average_lam, factor, matrix, coarse, kept):
    average = averaging()

    def last(z, carry):
        parts = products(matrix, wide0, z)
        for pair in range(4):
            cols = slice(pair * 256, pair * 256 + 256)
            value = middle[z + 1, :, cols] + STEP * combined(parts, pair)
            back = split_dot(value[0:64] + value[64:128], average)
            here = average_lam[z, pair]
            kept[z, pair] = here
            coarse[z, pair] = (back - here - factor[z, pair].astype(f32) * here).astype(bf16)
        return carry

    lax.fori_loop(0, 4, last, 0)


def gradient_body(scale, count, first, *refs):
    cots, wide, rest = refs[:count], refs[count], refs[count + 1 :]
    earlier, coarse, factor = rest[:3] if len(rest) == 6 else (None, None, None)
    out, widened_cot, total = rest[-3:]
    sums = jnp.zeros((128, 128), f32)
    zero = jnp.zeros((64, 256), bf16)
    for z in range(4):
        if count == 2:
            value = cots[z // 2][z % 2]
        else:
            value = cots[0][(z + 1) * 384 + 128 : (z + 1) * 384 + 256, :]
        widened_cot[z, 0:128] = value
        widened_cot[z, 128:192] = jnp.concatenate([zero, value[64:128, :768]], 1)
        widened_cot[z, 192:256] = jnp.concatenate([value[0:64, 256:], zero], 1)
        for part in range(8):
            sums = sums + value[:, part * 128 : part * 128 + 128].astype(f32)
    total[...] = jnp.zeros_like(total)

    def plane(z, carry):
        base = pl.multiple_of((z + first) * 384, 384)
        total[...] += lax.dot_general(
            widened_cot[z],
            wide[pl.ds(base, 1152), :],
            (((1,), (1,)), ((), ())),
            preferred_element_type=f32,
        )
        return carry

    lax.fori_loop(0, 4, plane, 0)
    lower = lax.broadcasted_iota(jnp.int32, (64, 128), 1) < 64

    def give(block, value):
        if earlier is None:
            out[block] = value
        else:
            start = 256 + 64 * (block % 2)
            out[block // 2, start : start + 64] = ((value + earlier[block]) * scale).astype(bf16)

    for tap in range(9):
        cols = slice(tap * 128, tap * 128 + 128)
        rows = [total[64 * q : 64 * q + 64, cols] for q in range(4)]
        taps = [jnp.where(lower, rows[1], rows[3]), jnp.where(lower, rows[0], rows[1]), jnp.where(lower, rows[2], rows[0])]
        taps = [value + pltpu.roll(value, 64, 1) for value in taps]
        give(tap, jnp.where(lower, taps[0], taps[1]))
        if tap % 2 == 0:
            kept = taps[2]
        else:
            give(9 + tap // 2, jnp.where(lower, kept, taps[2]))
    give(13, kept)
    give(14, sums[0:64] + sums[64:128])
    give(15, jnp.zeros((64, 128), f32))
    if earlier is not None:
        for group in range(8):
            out[group, 0:128] = coarse[group]
            out[group, 128:256] = factor[group]


def gradient(scale, cots, wide, first, *extra):
    ins = [near(value) for value in (*cots, wide, *extra)]
    return run(
        functools.partial(gradient_body, scale, len(cots), first),
        "gradient",
        5,
        jax.ShapeDtypeStruct((8, 384, 128), bf16) if extra else pltpu.VMEM((16, 64, 128), f32),
        ins,
        [pltpu.VMEM((4, 256, 1024), bf16), pltpu.VMEM((256, 1152), f32)],
    )


def meet_body(mixed, out, shared):
    groups = mixed.shape[0]
    value = jnp.zeros((128, 128), f32)
    out[0] = value.astype(bf16)
    summed = mixed[0, 256:384].astype(f32)
    for group in range(groups - 1):
        value = value + mixed[group, 128:256].astype(f32) * value + mixed[group, 0:128].astype(f32)
        out[group + 1] = value.astype(bf16)
        summed = summed + mixed[group + 1, 256:384].astype(f32)
    summed = summed.astype(bf16)
    for slab in range(shared.shape[0]):
        shared[slab] = summed


def join_body(shared, carried, out):
    summed = shared[0].astype(f32)
    for slab in range(1, shared.shape[0]):
        summed = summed + shared[slab].astype(f32)
    summed = summed.astype(bf16)
    for group in range(out.shape[0]):
        out[group, 0:128] = carried[group]
        out[group, 128:256] = summed


def finish_body(lam, average_lam, joined, out, taps, offset, turn):
    fine = lax.broadcasted_iota(jnp.int32, (128, 256), 1)
    coarse = lax.broadcasted_iota(jnp.int32, (128, 256), 0)
    copies = jnp.where((fine == 2 * coarse) | (fine == 2 * coarse + 1), 1.0, 0.0).astype(bf16)

    def plane(z, carry):
        for pair in range(4):
            carried = joined[2 * z + pair // 2, 64 * (pair % 2) : 64 * (pair % 2) + 64]
            value = split_dot(carried.astype(f32) - average_lam[z, pair], copies)
            for half in range(2):
                for x in (2 * pair, 2 * pair + 1):
                    turn[half, pl.ds(x, 64, stride=8), :] = value[:, half * 128 : half * 128 + 128]
        added = jnp.concatenate([turn[0], turn[1]], 1).reshape(64, 8, 256)
        out[:, z] = lam[:, z] + added
        return carry

    lax.fori_loop(0, 4, plane, 0)

    def block(index):
        start = 128 + 64 * (index % 2)
        return joined[index // 2, start : start + 64].astype(f32)

    for a in range(3):
        for c in range(3):
            tap = 3 * a + c
            both = block(tap)
            taps[9 * a + c] = both[:, :64]
            taps[9 * a + 3 + c] = both[:, 64:]
            half = 64 * (tap % 2)
            taps[9 * a + 6 + c] = block(9 + tap // 2)[:, half : half + 64]
    row = lax.broadcasted_iota(jnp.int32, (64, 64), 0)
    col = lax.broadcasted_iota(jnp.int32, (64, 64), 1)
    column = jnp.broadcast_to(jnp.sum(block(14), axis=1, keepdims=True), (64, 64))
    offset[...] = jnp.sum(jnp.where(row == col, column, 0.0), axis=0, keepdims=True)


def prepare_body(mask, weight, bias, matrix, flipped, offset, diag):
    row = lax.broadcasted_iota(jnp.int32, (64, 64), 0)
    col = lax.broadcasted_iota(jnp.int32, (64, 64), 1)
    zero = jnp.zeros((64, 64), f32)

    def column(values):
        return jnp.sum(jnp.where(row == col, values, 0.0), axis=1, keepdims=True)

    def build(out, tap):
        for a in range(3):
            for c in range(3):
                taps = [tap(9 * a + 3 * b + c) for b in range(3)]
                sides = ((taps[1], taps[2]), (taps[0], taps[1]), (taps[2], zero), (zero, taps[0]))
                start = (3 * a + c) * 128
                for place in range(4):
                    both = jnp.concatenate(sides[place], 1)
                    out[64 * place : 64 * place + 64, start : start + 128] = both.astype(bf16)

    build(matrix, lambda tap: weight[tap].astype(f32))
    build(flipped, lambda tap: weight[26 - tap].astype(f32).T)
    column_bias = jnp.broadcast_to(column(jnp.broadcast_to(bias[...], (64, 64))), (64, 256))
    offset[0:64] = column_bias
    offset[64:128] = column_bias
    diag[...] = jnp.broadcast_to(2.0 * STEP * column(weight[13].astype(f32)), (64, 128))


def neighbours(low_part, high_part):
    count = lax.axis_size("slab")
    up = [(i, i + 1) for i in range(count - 1)]
    down = [(i + 1, i) for i in range(count - 1)]
    return lax.ppermute(high_part, "slab", up), lax.ppermute(low_part, "slab", down)


def exchanged(value, axes):
    return lax.all_to_all(value, axes, 0, 0, tiled=True)


def on_device(u_states, lam_points, weight, bias):
    u, lam = u_states[0], lam_points[0]
    slab, slabs = lax.axis_index("slab"), lax.axis_size("slab")
    groups = lax.axis_size("tm")
    half = field(2, bf16)
    ones = jnp.ones((4,), f32)
    mask = jnp.concatenate([(slab > 0).astype(f32)[None], ones, (slab < slabs - 1).astype(f32)[None]])
    u_low, u_high = run(open_body, "open", 3, (half, half), [u], [TURN])
    u_lo, u_hi = neighbours(u_low, u_high)
    taps = pltpu.VMEM((256, 1152), bf16)
    matrix, flipped, offset, diag = run(
        prepare_body,
        "prepare",
        2,
        (taps, taps, pltpu.VMEM((128, 256), f32), pltpu.VMEM((64, 128), f32)),
        [mask, weight, bias[None]],
        scalars=1,
    )
    matrix, flipped, offset, diag = (near(v) for v in (matrix, flipped, offset, diag))
    coarse_shape = pltpu.VMEM((4, 4, 64, 128), bf16)
    average_shape = (4, 4, 64, 128)
    wide0, wide1, sens, lam_rows, average_lam = run(
        inner_body,
        "inner",
        5,
        (
            widened(8),
            widened(6),
            field(6, f32),
            field(4, f32),
            pltpu.VMEM(average_shape, f32),
        ),
        [near(u_low), near(u_high), lam, matrix, offset],
        [TURN],
    )
    wide0, wide1, sens, cot_low, cot_high, factor = run(
        forward_body,
        "forward",
        10,
        (widened(8), widened(6), field(6, f32), field(3, bf16), field(3, bf16), coarse_shape),
        [mask]
        + [near(v) for v in (wide0, wide1, sens, u_lo, u_hi, lam_rows)]
        + [matrix, offset, diag],
        aliases={1: 0, 2: 1, 3: 2},
        scalars=1,
    )
    cot_lo, cot_hi = neighbours(cot_low, cot_high)
    scale = STEP / math.sqrt(2 * groups * slabs * 4 * 8 * 256)
    earlier = gradient(scale, (cot_low, cot_high), wide1, 0)
    back1, back0, middle = run(
        back_inner_body,
        "back_inner",
        3,
        (widened(8), widened(6), field(6, f32)),
        [near(v) for v in (cot_low, cot_high, lam_rows, sens)] + [flipped],
    )
    back1, back0, middle = run(
        back_outer_body,
        "back_outer",
        5,
        (widened(8), widened(6), field(6, f32)),
        [mask]
        + [near(v) for v in (back1, back0, middle, cot_lo, cot_hi, lam_rows, sens)]
        + [flipped],
        aliases={1: 0, 2: 1, 3: 2},
        scalars=1,
    )
    coarse, average_lam = run(
        back_last_body,
        "back_last",
        5,
        (coarse_shape, jax.ShapeDtypeStruct(average_shape, f32)),
        [near(v) for v in (back0, middle, average_lam, factor)] + [flipped],
    )
    pieces = (groups, 128, 128)
    mixed = gradient(scale, (back0,), wide0, 1, earlier, coarse.reshape(pieces), factor.reshape(pieces))
    carried, shared = run(
        meet_body,
        "meet",
        1,
        (jax.ShapeDtypeStruct(pieces, bf16), jax.ShapeDtypeStruct((slabs, 128, 128), bf16)),
        [exchanged(mixed, "tm")],
    )
    joined = run(
        join_body,
        "join",
        1,
        jax.ShapeDtypeStruct((groups, 256, 128), bf16),
        [exchanged(shared, "slab"), carried],
    )
    updated, taps, offset = run(
        finish_body,
        "finish",
        4,
        (
            jax.ShapeDtypeStruct(lam.shape, f32),
            jax.ShapeDtypeStruct(weight.shape, f32),
            jax.ShapeDtypeStruct((1, 64), f32),
        ),
        [lam, average_lam, exchanged(joined, "tm")],
        [TURN],
    )
    return updated[None], taps, offset[0]


def solution(mesh):
    in_specs = (P("tm", None, "slab", None, None), P("tm", None, "slab", None, None), P(), P())
    out_specs = (P("tm", None, "slab", None, None), P(), P())
    return jax.shard_map(
        on_device, mesh=mesh, in_specs=in_specs, out_specs=out_specs, check_vma=False
    )
```

time: 162 us -> 112 us (0.69)
  blocking collectives: 0 us -> 54.2 us
  starting transfers between devices: 52.8 us -> 12.9 us
  waiting for transfers between devices: 31.8 us -> 1.94 us
  Pallas kernels: 55.7 us -> 38.9 us
  local copies, waits for them, and re-layouts: 17 us -> 2.24 us
  other arithmetic: 2.63 us -> 0.08 us
    all_to_all x0 -> x3, blocking collectives: none -> 54.2 us  [exchanged(): return lax.all_to_all(value, axes, 0, 0, tiled=True)]
    all_to_all x5 -> x0, starting transfers between devices: 36.3 us -> none  [exchanged(): return lax.all_to_all(value, axes, 0, 0, tiled=True)]
    all_to_all x5 -> x0, waiting for transfers between devices: 28.5 us -> none  [exchanged(): return lax.all_to_all(value, axes, 0, 0, tiled=True)]
    pallas_call x7 -> x12, Pallas kernels: 55.7 us -> 38.9 us  [run(): pl.pallas_call(body, out_shape=outs, in_specs=in_specs, scratch_shapes=li...]
    slice x5 -> x0, local copies, waits for them, and re-layouts: 5.63 us -> none  [the longest x1 2.41 us: on_device(): cot_lo, cot_hi = neighbours(cot1[:2], cot1[2:])]
    reshape x2 -> x0, local copies, waits for them, and re-layouts: 3.02 us -> none  [tap_matrix(): return jnp.stack([even, odd], 4).reshape(256, 1152)]
    ppermute x3 -> x2, starting transfers between devices: 10.2 us -> 7.55 us  [neighbours(): lax.ppermute(high_part, 'slab', up)]
    ppermute x3 -> x2, waiting for transfers between devices: 3.24 us -> 0.75 us  [neighbours(): lax.ppermute(low_part, 'slab', down)]
  transfers between devices with their start and end apart: 11 -> 4, of which waited for: 4 -> 2; matrix products, arithmetic and copies ran while one was open for 6% -> 0% of each run, Pallas kernels for 23% -> 11%
where the time goes in v2:
time: 112 us; the launch traced here: 111 us
  blocking collectives  54.2 us (48%)
  Pallas kernels  38.9 us (35%)
  starting transfers between devices  12.9 us (12%)
  local copies, waits for them, and re-layouts  2.24 us (2%)
  waiting for transfers between devices  1.94 us (2%)
    all_to_all x3, blocking collectives, exchanged(): return lax.all_to_all(value, axes, 0, 0, tiled=True)  54.2 us
    pallas_call x12, Pallas kernels, run(): pl.pallas_call(body, out_shape=outs, in_specs=in_specs, scratch_shapes=li...  38.9 us
    ppermute x2, starting transfers between devices, neighbours(): lax.ppermute(high_part, 'slab', up)  7.55 us
    ppermute x2, starting transfers between devices, neighbours(): lax.ppermute(low_part, 'slab', down)  5.37 us
    unnamed x8, local copies, waits for them, and re-layouts  2.24 us
  transfers between devices with their start and end apart: 4, of which 2 were waited for; matrix products, arithmetic and copies ran while one was open for 0% of the time, Pallas kernels for 11%

profile of v2, /device:TPU:1, one launch (start us, length us, event | category | flops | bytes accessed | tf_op | source)
XLA Modules:
  0.0 111.0 jit_solution(6587412977166180824)
XLA Ops:
  0.6 0.0 copy-start.1
  0.6 1.2 %copy-done.1 = bf16[1,64,4,8,256]{4,3,2,1,0:T(8,128)(2,1)S(1)} copy-done((bf16[1,64,4,8,256]{4,3,2,1,0:T(8,128)(2,1)S(1)}, bf16[1,64,4,8,256]{4,3,2,1,0:T(8,128)(2,1)}, u32[]{:S(2)}) %copy-start.1) | copy-done | bytes 1048600
  1.9 0.0 copy-start.3
  1.9 1.4 %open.1 = (bf16[2,128,1024]{2,1,0:T(8,128)(2,1)}, bf16[2,128,1024]{2,1,0:T(8,128)(2,1)}) custom-call(bf16[64,4,8,256]{3,2,1,0:T(8,128)(2,1)S(1)} %bitcast.11), custom_call_target="tpu_custom_call" | custom-call | flops 3300000000 | tf_op jit(solution)/shard_map/open/pallas_call | solution.py:97
  3.2 0.0 copy-start
  3.2 3.4 %collective-permute-start.1 = (bf16[2,128,1024]{2,1,0:T(8,128)(2,1)}, bf16[2,128,1024]{2,1,0:T(8,128)(2,1)S(1)}, u32[]{:S(2)}, u32[]{:S(2)}) collective-permute-start(bf16[2,128,1024]{2,1,0:T(8,128)(2,1)} %get-tuple-element.32.low), channel_id=1, source_target_pairs={{1,0},{2,1},{3,2},{4,3},{5,4},{6,5},{7,6},{8,7},{9,8},{10,9},{11,1... | collective-permute-start | bytes 1572872 | tf_op jit(solution)/shard_map/ppermute | solution.py:413
  6.7 3.5 %collective-permute-start = (bf16[2,128,1024]{2,1,0:T(8,128)(2,1)}, bf16[2,128,1024]{2,1,0:T(8,128)(2,1)S(1)}, u32[]{:S(2)}, u32[]{:S(2)}) collective-permute-start(bf16[2,128,1024]{2,1,0:T(8,128)(2,1)} %get-tuple-element.33.high), channel_id=1, source_target_pairs={{0,1},{1,2},{2,3},{3,4},{4,5},{5,6},{6,7},{7,8},{8,9},{9,10},{10,1... | collective-permute-start | bytes 1572872 | tf_op jit(solution)/shard_map/ppermute | solution.py:413
  10.2 0.1 pad_maximum_fusion.mask
  10.3 0.0 copy-done.3
  10.3 0.0 copy-start.2
  10.3 1.0 copy-done.2
  11.3 1.1 prepare.1
  12.4 0.0 copy-done
  12.4 4.6 %inner.1 = (bf16[3072,1024]{1,0:T(8,128)(2,1)S(1)}, bf16[2304,1024]{1,0:T(8,128)(2,1)S(1)}, f32[6,128,1024]{2,1,0:T(8,128)S(1)}, f32[4,128,1024]{2,1,0:T(8,128)S(1)}, f32[4,4,64,128]{3,2,1,0:T(8,128)S(1)}) custom-call(bf16[2,128,1024]{2,1,0:T(8,128)(2,1)} %get-tuple-element.32.low, bf16[2,128,1024]{2,1,0:T(8,128)(2,1)} %get-tuple-element.33.high, ...), custom_call_target="tpu_custom_call" | custom-call | flops 5500000256 | tf_op jit(solution)/shard_map/inner/pallas_call | solution.py:97
  17.1 0.0 collective-permute-done.1.u_hi
  17.1 0.0 collective-permute-done.u_lo
  17.1 8.9 %forward.1 = (bf16[3072,1024]{1,0:T(8,128)(2,1)S(1)}, bf16[2304,1024]{1,0:T(8,128)(2,1)S(1)}, f32[6,128,1024]{2,1,0:T(8,128)S(1)}, bf16[3,128,1024]{2,1,0:T(8,12...) custom-call(f32[6]{0:T(128)S(1)} %pad_maximum_fusion.mask, ...), custom_call_target="tpu_custom_call", output_to_operand_aliasing={{0}: (1, {}), {1}: (2, {}), {2}: (3, {})} | custom-call | flops 11000000512 | tf_op jit(solution)/shard_map/forward/pallas_call | solution.py:97
  26.0 1.9 %collective-permute-start.3 = (bf16[3,128,1024]{2,1,0:T(8,128)(2,1)S(1)}, bf16[3,128,1024]{2,1,0:T(8,128)(2,1)S(1)}, u32[]{:S(2)}, u32[]{:S(2)}) collective-permute-start(bf16[3,128,1024]{2,1,0:T(8,128)(2,1)S(1)} %get-tuple-element.41.low.refs_0_), channel_id=1, source_target_pairs={{1,0},{2,1},{3,2},{4,3},{5,4},{6,5},{7,6},{8,7},{9,8},{10,9},{11,1... | collective-permute-start | bytes 2359304 | tf_op jit(solution)/shard_map/ppermute | solution.py:413
  27.9 4.0 %collective-permute-start.2 = (bf16[3,128,1024]{2,1,0:T(8,128)(2,1)S(1)}, bf16[3,128,1024]{2,1,0:T(8,128)(2,1)S(1)}, u32[]{:S(2)}, u32[]{:S(2)}) collective-permute-start(bf16[3,128,1024]{2,1,0:T(8,128)(2,1)S(1)} %get-tuple-element.42.high.refs_1_), channel_id=1, source_target_pairs={{0,1},{1,2},{2,3},{3,4},{4,5},{5,6},{6,7},{7,8},{8,9},{9,10},{10,1... | collective-permute-start | bytes 2359304 | tf_op jit(solution)/shard_map/ppermute | solution.py:413
  31.9 2.6 %back_inner.1 = (bf16[3072,1024]{1,0:T(8,128)(2,1)S(1)}, bf16[2304,1024]{1,0:T(8,128)(2,1)S(1)}, f32[6,128,1024]{2,1,0:T(8,128)S(1)}) custom-call(bf16[3,128,1024]{2,1,0:T(8,128)(2,1)S(1)} %get-tuple-element.41.low.refs_0_, bf16[3,128,1024]{2,1,0:T(8,128)(2,1)S(1)} %get-tuple-element.42.high.refs_1_, f32[4,128,1024]{2,1,0:T(8,128)S(1)} %get-tuple-element.39.lam, ...), custom_call_target="tpu_custom_call" | custom-call | flops 3300000000 | tf_op jit(solution)/shard_map/back_inner/pallas_call | solution.py:97
  34.6 4.2 %gradient.2.refs_2_ = f32[16,64,128]{2,1,0:T(8,128)S(1)} custom-call(bf16[3,128,1024]{2,1,0:T(8,128)(2,1)S(1)} %get-tuple-element.41.low.refs_0_, bf16[3,128,1024]{2,1,0:T(8,128)(2,1)S(1)} %get-tuple-element.42.high.refs_1_, bf16[2304,1024]{1,0:T(8,128)(2,1)S(1)} %get-tuple-element.54.refs_2_), custom_call_target="tpu_custom_call" | custom-call | flops 5500000256 | tf_op jit(solution)/shard_map/gradient/pallas_call | solution.py:97
  38.7 0.8 collective-permute-done.3.cot_hi
  39.5 1.2 %collective-permute-done.2.cot_lo = bf16[3,128,1024]{2,1,0:T(8,128)(2,1)S(1)} collective-permute-done((bf16[3,128,1024]{2,1,0:T(8,128)(2,1)S(1)}, bf16[3,128,1024]{2,1,0:T(8,128)(2,1)S(1)}, u32[]{:S(2)}, u32[]{:S(2)}) %collective-permute-start.2) | collective-permute-done | bytes 786464 | tf_op jit(solution)/shard_map/ppermute | solution.py:413
  40.7 4.5 %back_outer.1 = (bf16[3072,1024]{1,0:T(8,128)(2,1)S(1)}, bf16[2304,1024]{1,0:T(8,128)(2,1)S(1)}, f32[6,128,1024]{2,1,0:T(8,128)S(1)}) custom-call(f32[6]{0:T(128)S(1)} %pad_maximum_fusion.mask, bf16[3072,1024]{1,0:T(8,128)(2,1)S(1)} %get-tuple-element.45.wide1_in, ...), custom_call_target="tpu_custom_call", output_to_operand_aliasing={{0}: (1, {}), {1}: (2, {}), {2}: (3, {})} | custom-call | flops 5500000256 | tf_op jit(solution)/shard_map/back_outer/pallas_call | solution.py:97
  45.2 4.3 %back_last.1 = (bf16[4,4,64,128]{3,2,1,0:T(8,128)(2,1)S(1)}, f32[4,4,64,128]{3,2,1,0:T(8,128)S(1)}) custom-call(bf16[2304,1024]{1,0:T(8,128)(2,1)S(1)} %get-tuple-element.48.wide0.refs_0_, f32[6,128,1024]{2,1,0:T(8,128)S(1)} %get-tuple-element.49.middle, f32[4,4,64,128]{3,2,1,0:T(8,128)S(1)} %get-tuple-element.50.average_lam, ...), custom_call_target="tpu_custom_call" | custom-call | flops 5500000256 | tf_op jit(solution)/shard_map/back_last/pallas_call | solution.py:97
  49.5 4.2 %gradient.3 = bf16[8,384,128]{2,1,0:T(8,128)(2,1)S(1)} custom-call(bf16[2304,1024]{1,0:T(8,128)(2,1)S(1)} %get-tuple-element.48.wide0.refs_0_, bf16[3072,1024]{1,0:T(8,128)(2,1)S(1)} %get-tuple-element.53.refs_1_, f32[16,64,128]{2,1,0:T(8,128)S(1)} %gradient.2.refs_2_, bf16[8,128,128]{2,1,0:T(8,128)(2,1)S(1)} %bitcast.14, bf16[8,128,128]{2,1,0:T(8,128)(2,1)S(1)} %bitcast.13), custom_call_target="tpu_custom_call" | custom-call | flops 5500000256 | tf_op jit(solution)/shard_map/gradient/pallas_call | solution.py:97
  53.7 15.4 %all_to_all.15.mixed = bf16[8,384,128]{2,1,0:T(8,128)(2,1)S(1)} all-to-all(bf16[8,384,128]{2,1,0:T(8,128)(2,1)S(1)} %gradient.3), channel_id=1, replica_groups=mesh['tm'=8,'slab'=16] {'tm'}, dimensions={0} | all-to-all | bytes 1572864 | tf_op jit(solution)/shard_map/all_to_all | solution.py:417
  69.1 0.1 meet.1
  69.2 27.4 %all_to_all.16.shared = bf16[16,128,128]{2,1,0:T(8,128)(2,1)S(1)} all-to-all(bf16[16,128,128]{2,1,0:T(8,128)(2,1)S(1)} %get-tuple-element.56), channel_id=1, replica_groups=mesh['tm'=8,'slab'=16] {'slab'}, dimensions={0} | all-to-all | bytes 1048576 | tf_op jit(solution)/shard_map/all_to_all | solution.py:417
  96.6 0.1 join.1
  96.7 11.4 %all_to_all.17.joined = bf16[8,256,128]{2,1,0:T(8,128)(2,1)S(1)} all-to-all(bf16[8,256,128]{2,1,0:T(8,128)(2,1)S(1)} %join.1), channel_id=1, replica_groups=mesh['tm'=8,'slab'=16] {'tm'}, dimensions={0} | all-to-all | bytes 1048576 | tf_op jit(solution)/shard_map/all_to_all | solution.py:417
  108.1 2.9 %finish.1 = (f32[64,4,8,256]{3,2,1,0:T(8,128)}, f32[27,64,64]{2,1,0:T(8,128)}, f32[1,64]{1,0:T(1,128)}) custom-call(f32[64,4,8,256]{3,2,1,0:T(8,128)S(1)} %bitcast.10, f32[4,4,64,128]{3,2,1,0:T(8,128)S(1)} %get-tuple-element.52.average_lam, bf16[8,256,128]{2,1,0:T(8,128)(2,1)S(1)} %all_to_all.17.joined), custom_call_target="tpu_custom_call" | custom-call | flops 4400000000 | tf_op jit(solution)/shard_map/finish/pallas_call | solution.py:97
  (1 shorter events, 0.0 us)
Async XLA Ops:
  0.6 1.2 %copy-start.1 = (bf16[1,64,4,8,256]{4,3,2,1,0:T(8,128)(2,1)S(1)}, bf16[1,64,4,8,256]{4,3,2,1,0:T(8,128)(2,1)}, u32[]{:S(2)}) copy-start(bf16[1,64,4,8,256]{4,3,2,1,0:T(8,128)(2,1)} %param.4) | copy-start | bytes 3145732
  1.9 8.5 %copy-start.3 = (f32[64]{0:T(128)S(1)}, f32[64]{0:T(128)}, u32[]{:S(2)}) copy-start(f32[64]{0:T(128)} %param.7) | copy-start | bytes 772
  3.2 9.2 %copy-start = (f32[1,64,4,8,256]{4,3,2,1,0:T(8,128)S(1)}, f32[1,64,4,8,256]{4,3,2,1,0:T(8,128)}, u32[]{:S(2)}) copy-start(f32[1,64,4,8,256]{4,3,2,1,0:T(8,128)} %param.5) | copy-start | bytes 6291460
  3.2 13.8 %collective-permute-start.1 = (bf16[2,128,1024]{2,1,0:T(8,128)(2,1)}, bf16[2,128,1024]{2,1,0:T(8,128)(2,1)S(1)}, u32[]{:S(2)}, u32[]{:S(2)}) collective-permute-start(bf16[2,128,1024]{2,1,0:T(8,128)(2,1)} %get-tuple-element.32.low), channel_id=1, source_target_pairs={{1,0},{2,1},{3,2},{4,3},{5,4},{6,5},{7,6},{8,7},{9,8},{10,9},{11,1... | collective-permute-start | bytes 1572872 | tf_op jit(solution)/shard_map/ppermute | solution.py:413
  6.7 10.4 %collective-permute-start = (bf16[2,128,1024]{2,1,0:T(8,128)(2,1)}, bf16[2,128,1024]{2,1,0:T(8,128)(2,1)S(1)}, u32[]{:S(2)}, u32[]{:S(2)}) collective-permute-start(bf16[2,128,1024]{2,1,0:T(8,128)(2,1)} %get-tuple-element.33.high), channel_id=1, source_target_pairs={{0,1},{1,2},{2,3},{3,4},{4,5},{5,6},{6,7},{7,8},{8,9},{9,10},{10,1... | collective-permute-start | bytes 1572872 | tf_op jit(solution)/shard_map/ppermute | solution.py:413
  10.3 1.0 copy-start.2
  26.0 13.5 %collective-permute-start.3 = (bf16[3,128,1024]{2,1,0:T(8,128)(2,1)S(1)}, bf16[3,128,1024]{2,1,0:T(8,128)(2,1)S(1)}, u32[]{:S(2)}, u32[]{:S(2)}) collective-permute-start(bf16[3,128,1024]{2,1,0:T(8,128)(2,1)S(1)} %get-tuple-element.41.low.refs_0_), channel_id=1, source_target_pairs={{1,0},{2,1},{3,2},{4,3},{5,4},{6,5},{7,6},{8,7},{9,8},{10,9},{11,1... | collective-permute-start | bytes 2359304 | tf_op jit(solution)/shard_map/ppermute | solution.py:413
  27.9 12.8 %collective-permute-start.2 = (bf16[3,128,1024]{2,1,0:T(8,128)(2,1)S(1)}, bf16[3,128,1024]{2,1,0:T(8,128)(2,1)S(1)}, u32[]{:S(2)}, u32[]{:S(2)}) collective-permute-start(bf16[3,128,1024]{2,1,0:T(8,128)(2,1)S(1)} %get-tuple-element.42.high.refs_1_), channel_id=1, source_target_pairs={{0,1},{1,2},{2,3},{3,4},{4,5},{5,6},{6,7},{7,8},{8,9},{9,10},{10,1... | collective-permute-start | bytes 2359304 | tf_op jit(solution)/shard_map/ppermute | solution.py:413

commit v3 on v2

--- a/solution.py
+++ b/solution.py
@@ -23,7 +23,7 @@
 def put(wide, plane, row, pair, value):
     count = value.shape[0]
     left, right = shifts(value)
-    base = plane * 384 + row
+    base = pl.multiple_of(plane * 384 + row, 64)
     cols = slice(pair * 256, pair * 256 + 256)
     wide[pl.ds(base, count), cols] = left
     wide[pl.ds(base + 128, count), cols] = value
@@ -109,12 +109,23 @@
 TURN = pltpu.VMEM((2, 512, 128), f32)
 
 
-def open_body(u, low, high, turn):
-    for z in range(4):
-        to_rows(u, z, turn)
-        target = low if z < 2 else high
+def sides(spot):
+    odd = spot[0]
+    return 2 * (1 - odd), 2 * odd
+
+
+def open_body(spot, u, out_a, out_b, turn):
+    for base, target in zip(sides(spot), (out_a, out_b)):
+        for place in range(2):
+            to_rows(u, base + place, turn)
+            for pair in range(4):
+                target[place, :, pair * 256 : pair * 256 + 256] = pair_of(turn, pair).astype(bf16)
+
+
+def put_planes(wide, z, source):
+    for place in range(2):
         for pair in range(4):
-            target[z % 2, :, pair * 256 : pair * 256 + 256] = pair_of(turn, pair).astype(bf16)
+            put(wide, z + place, 0, pair, source[place, :, pair * 256 : pair * 256 + 256])
 
 
 def step_state(z, matrix, offset, wide0, wide1, sens, weight):
@@ -130,12 +141,10 @@
         put(wide1, z, 0, pair, value.astype(bf16))
 
 
-def inner_body(low, high, lam, matrix, bias, wide0, wide1, sens, lam_rows, average_lam, turn):
+def inner_body(spot, own_a, own_b, lam, matrix, bias, wide0, wide1, sens, lam_rows, average_lam, turn):
     average = averaging()
-    for z in range(4):
-        source = low if z < 2 else high
-        for pair in range(4):
-            put(wide0, z + 2, 0, pair, source[z % 2, :, pair * 256 : pair * 256 + 256])
+    for base, source in zip(sides(spot), (own_a, own_b)):
+        put_planes(wide0, base + 2, source)
     offset = bias[...]
 
     def inside(z, carry):
@@ -152,12 +161,9 @@
             average_lam[z, pair] = split_dot(value[0:64] + value[64:128], average)
 
 
-def forward_body(mask, wide0_in, wide1_in, sens_in, u_lo, u_hi, lam, matrix, bias, diag, wide0, wide1, sens, cot_low, cot_high, factor):
-    for z in range(2):
-        for pair in range(4):
-            cols = slice(pair * 256, pair * 256 + 256)
-            put(wide0, z, 0, pair, u_lo[z, :, cols])
-            put(wide0, z + 6, 0, pair, u_hi[z, :, cols])
+def forward_body(spot, mask, wide0_in, wide1_in, sens_in, u_a, u_b, lam, matrix, bias, diag, wide0, wide1, sens, cot_a, cot_b, factor):
+    for base, source in zip(sides(spot), (u_a, u_b)):
+        put_planes(wide0, 3 * base, source)
     offset = bias[...]
 
     def outside(index, carry):
@@ -178,18 +184,14 @@
             coarse = jnp.dot(both.astype(bf16), average, preferred_element_type=f32)
             factor[z, pair] = (coarse * diag[...]).astype(bf16)
 
-    def second_low(z, carry):
-        second(z, cot_low, z)
-        return carry
-
-    def second_high(z, carry):
-        second(z + 2, cot_high, z)
-        return carry
-
-    cot_low[2] = lam[0].astype(bf16)
-    cot_high[2] = lam[3].astype(bf16)
-    lax.fori_loop(0, 2, second_low, 0)
-    lax.fori_loop(0, 2, second_high, 0)
+    for base, target in zip(sides(spot), (cot_a, cot_b)):
+        target[2] = lam[base + base // 2].astype(bf16)
+
+        def plane(place, carry, base=base, target=target):
+            second(base + place, target, place)
+            return carry
+
+        lax.fori_loop(0, 2, plane, 0)
 
 
 def step_back(z, matrix, wide1, wide0, middle, sens, lam, weight):
@@ -204,11 +206,9 @@
         put(wide0, z, 0, pair, value.astype(bf16))
 
 
-def back_inner_body(low, high, lam, sens, matrix, wide1, wide0, middle):
-    for z in range(4):
-        source = low if z < 2 else high
-        for pair in range(4):
-            put(wide1, z + 2, 0, pair, source[z % 2, :, pair * 256 : pair * 256 + 256])
+def back_inner_body(spot, own_a, own_b, lam, sens, matrix, wide1, wide0, middle):
+    for base, source in zip(sides(spot), (own_a, own_b)):
+        put_planes(wide1, base + 2, source)
 
     def inside(z, carry):
         step_back(z, matrix, wide1, wide0, middle, sens, lambda cols: lam[z - 1, :, cols], None)
@@ -217,21 +217,19 @@
     lax.fori_loop(2, 4, inside, 0)
 
 
-def back_outer_body(mask, wide1_in, wide0_in, middle_in, cot_lo, cot_hi, lam, sens, matrix, wide1, wide0, middle):
-    for z in range(2):
-        for pair in range(4):
-            cols = slice(pair * 256, pair * 256 + 256)
-            put(wide1, z, 0, pair, cot_lo[z, :, cols])
-            put(wide1, z + 6, 0, pair, cot_hi[z, :, cols])
+def back_outer_body(spot, mask, wide1_in, wide0_in, middle_in, cot_a, cot_b, lam, sens, matrix, wide1, wide0, middle):
+    for base, source in zip(sides(spot), (cot_a, cot_b)):
+        put_planes(wide1, 3 * base, source)
 
     def outside(index, carry):
         z = 1 + 3 * index
         step_back(z, matrix, wide1, wide0, middle, sens, lambda cols: lam[z - 1, :, cols], None)
         return carry
 
-    step_back(0, matrix, wide1, wide0, middle, sens, lambda cols: cot_lo[2, :, cols].astype(f32), mask[0])
     lax.fori_loop(0, 2, outside, 0)
-    step_back(5, matrix, wide1, wide0, middle, sens, lambda cols: cot_hi[2, :, cols].astype(f32), mask[5])
+    for base, source in zip(sides(spot), (cot_a, cot_b)):
+        z = 2 * base + base // 2
+        step_back(z, matrix, wide1, wide0, middle, sens, lambda cols: source[2, :, cols].astype(f32), mask[z])
 
 
 def back_last_body(wide0, middle, average_lam, factor, matrix, coarse, kept):
@@ -251,17 +249,21 @@
     lax.fori_loop(0, 4, last, 0)
 
 
-def gradient_body(scale, count, first, *refs):
-    cots, wide, rest = refs[:count], refs[count], refs[count + 1 :]
-    earlier, coarse, factor = rest[:3] if len(rest) == 6 else (None, None, None)
-    out, widened_cot, total = rest[-3:]
+def gradient_body(scale, spot, *refs):
+    last = len(refs) == 8
+    cots, wide, rest = (refs[:1], refs[1], refs[2:]) if last else (refs[:2], refs[2], refs[3:])
+    if last:
+        earlier, mine, others, out, widened_cot, total = rest
+    else:
+        out, widened_cot, total = rest
     sums = jnp.zeros((128, 128), f32)
     zero = jnp.zeros((64, 256), bf16)
+    side_a, side_b = sides(spot)
     for z in range(4):
-        if count == 2:
+        if last:
+            value = cots[0][(z + 1) * 384 + 128 : (z + 1) * 384 + 256, :]
+        else:
             value = cots[z // 2][z % 2]
-        else:
-            value = cots[0][(z + 1) * 384 + 128 : (z + 1) * 384 + 256, :]
         widened_cot[z, 0:128] = value
         widened_cot[z, 128:192] = jnp.concatenate([zero, value[64:128, :768]], 1)
         widened_cot[z, 192:256] = jnp.concatenate([value[0:64, 256:], zero], 1)
@@ -270,7 +272,8 @@
     total[...] = jnp.zeros_like(total)
 
     def plane(z, carry):
-        base = pl.multiple_of((z + first) * 384, 384)
+        above = z + 1 if last else jnp.where(z < 2, side_a, side_b) + z % 2
+        base = pl.multiple_of(above * 384, 384)
         total[...] += lax.dot_general(
             widened_cot[z],
             wide[pl.ds(base, 1152), :],
@@ -283,11 +286,7 @@
     lower = lax.broadcasted_iota(jnp.int32, (64, 128), 1) < 64
 
     def give(block, value):
-        if earlier is None:
-            out[block] = value
-        else:
-            start = 256 + 64 * (block % 2)
-            out[block // 2, start : start + 64] = ((value + earlier[block]) * scale).astype(bf16)
+        out[block] = (value + earlier[block]) * scale if last else value
 
     for tap in range(9):
         cols = slice(tap * 128, tap * 128 + 128)
@@ -302,49 +301,58 @@
     give(13, kept)
     give(14, sums[0:64] + sums[64:128])
     give(15, jnp.zeros((64, 128), f32))
-    if earlier is not None:
-        for group in range(8):
-            out[group, 0:128] = coarse[group]
-            out[group, 128:256] = factor[group]
-
-
-def gradient(scale, cots, wide, first, *extra):
-    ins = [near(value) for value in (*cots, wide, *extra)]
+    if last:
+        for block in range(8):
+            mine[block] = out[block + 8 * spot[0]]
+            others[block] = out[block + 8 - 8 * spot[0]]
+
+
+def gradient(scale, spot, cots, wide, earlier=None):
+    blocks, half = pltpu.VMEM((16, 64, 128), f32), pltpu.VMEM((8, 64, 128), f32)
+    ins = [*cots, wide] if earlier is None else [*cots, wide, earlier]
     return run(
-        functools.partial(gradient_body, scale, len(cots), first),
+        functools.partial(gradient_body, scale),
         "gradient",
         5,
-        jax.ShapeDtypeStruct((8, 384, 128), bf16) if extra else pltpu.VMEM((16, 64, 128), f32),
-        ins,
-        [pltpu.VMEM((4, 256, 1024), bf16), pltpu.VMEM((256, 1152), f32)],
-    )
+        blocks if earlier is None else (half, half),
+        [spot] + [near(value) for value in ins],
+        ([] if earlier is None else [blocks]) + [pltpu.VMEM((4, 256, 1024), bf16), pltpu.VMEM((256, 1152), f32)],
+        scalars=1,
+    )
+
+
+def pack_body(mine, received, coarse, factor, out):
+    for group in range(out.shape[0]):
+        out[group, 0:128] = coarse[group]
+        out[group, 128:256] = factor[group]
+        out[group, 256:320] = (mine[group] + received[group]).astype(bf16)
 
 
 def meet_body(mixed, out, shared):
     groups = mixed.shape[0]
     value = jnp.zeros((128, 128), f32)
     out[0] = value.astype(bf16)
-    summed = mixed[0, 256:384].astype(f32)
+    summed = mixed[0, 256:320].astype(f32)
     for group in range(groups - 1):
         value = value + mixed[group, 128:256].astype(f32) * value + mixed[group, 0:128].astype(f32)
         out[group + 1] = value.astype(bf16)
-        summed = summed + mixed[group + 1, 256:384].astype(f32)
+        summed = summed + mixed[group + 1, 256:320].astype(f32)
     summed = summed.astype(bf16)
-    for slab in range(shared.shape[0]):
-        shared[slab] = summed
+    for chip in range(shared.shape[0]):
+        shared[chip] = summed
 
 
 def join_body(shared, carried, out):
     summed = shared[0].astype(f32)
-    for slab in range(1, shared.shape[0]):
-        summed = summed + shared[slab].astype(f32)
+    for chip in range(1, shared.shape[0]):
+        summed = summed + shared[chip].astype(f32)
     summed = summed.astype(bf16)
     for group in range(out.shape[0]):
         out[group, 0:128] = carried[group]
-        out[group, 128:256] = summed
-
-
-def finish_body(lam, average_lam, joined, out, taps, offset, turn):
+        out[group, 128:192] = summed
+
+
+def finish_body(lam, average_lam, joined, out, turn):
     fine = lax.broadcasted_iota(jnp.int32, (128, 256), 1)
     coarse = lax.broadcasted_iota(jnp.int32, (128, 256), 0)
     copies = jnp.where((fine == 2 * coarse) | (fine == 2 * coarse + 1), 1.0, 0.0).astype(bf16)
@@ -362,9 +370,12 @@
 
     lax.fori_loop(0, 4, plane, 0)
 
+
+def taps_body(spot, joined, received, taps, offset):
     def block(index):
-        start = 128 + 64 * (index % 2)
-        return joined[index // 2, start : start + 64].astype(f32)
+        own = joined[index % 8, 128:192].astype(f32)
+        other = received[index % 8].astype(f32)
+        return jnp.where(spot[0] == index // 8, own, other)
 
     for a in range(3):
         for c in range(3):
@@ -406,11 +417,12 @@
     diag[...] = jnp.broadcast_to(2.0 * STEP * column(weight[13].astype(f32)), (64, 128))
 
 
-def neighbours(low_part, high_part):
+def neighbours(side_a, side_b):
     count = lax.axis_size("slab")
-    up = [(i, i + 1) for i in range(count - 1)]
-    down = [(i + 1, i) for i in range(count - 1)]
-    return lax.ppermute(high_part, "slab", up), lax.ppermute(low_part, "slab", down)
+    across = [(i, i + 1) for i in range(1, count - 1, 2)]
+    from_b = lax.ppermute(side_b, "slab", across + [(j, i) for i, j in across])
+    from_a = lax.ppermute(side_a, "slab", [(i, i ^ 1) for i in range(count)])
+    return from_a, from_b
 
 
 def exchanged(value, axes):
@@ -424,8 +436,9 @@
     half = field(2, bf16)
     ones = jnp.ones((4,), f32)
     mask = jnp.concatenate([(slab > 0).astype(f32)[None], ones, (slab < slabs - 1).astype(f32)[None]])
-    u_low, u_high = run(open_body, "open", 3, (half, half), [u], [TURN])
-    u_lo, u_hi = neighbours(u_low, u_high)
+    spot = (slab % 2).astype(jnp.int32)[None]
+    own_a, own_b = run(open_body, "open", 3, (half, half), [spot, u], [TURN], scalars=1)
+    u_a, u_b = neighbours(own_a, own_b)
     taps = pltpu.VMEM((256, 1152), bf16)
     matrix, flipped, offset, diag = run(
         prepare_body,
@@ -449,41 +462,46 @@
             field(4, f32),
             pltpu.VMEM(average_shape, f32),
         ),
-        [near(u_low), near(u_high), lam, matrix, offset],
+        [spot, near(own_a), near(own_b), lam, matrix, offset],
         [TURN],
-    )
-    wide0, wide1, sens, cot_low, cot_high, factor = run(
+        scalars=1,
+    )
+    wide0, wide1, sens, own_a, own_b, factor = run(
         forward_body,
         "forward",
         10,
         (widened(8), widened(6), field(6, f32), field(3, bf16), field(3, bf16), coarse_shape),
-        [mask]
-        + [near(v) for v in (wide0, wide1, sens, u_lo, u_hi, lam_rows)]
+        [spot, mask]
+        + [near(v) for v in (wide0, wide1, sens, u_a, u_b, lam_rows)]
         + [matrix, offset, diag],
-        aliases={1: 0, 2: 1, 3: 2},
-        scalars=1,
-    )
-    cot_lo, cot_hi = neighbours(cot_low, cot_high)
+        aliases={2: 0, 3: 1, 4: 2},
+        scalars=2,
+    )
+    cot_a, cot_b = neighbours(own_a, own_b)
     scale = STEP / math.sqrt(2 * groups * slabs * 4 * 8 * 256)
-    earlier = gradient(scale, (cot_low, cot_high), wide1, 0)
+    earlier = gradient(scale, spot, (own_a, own_b), wide1)
     back1, back0, middle = run(
         back_inner_body,
         "back_inner",
         3,
         (widened(8), widened(6), field(6, f32)),
-        [near(v) for v in (cot_low, cot_high, lam_rows, sens)] + [flipped],
+        [spot] + [near(v) for v in (own_a, own_b, lam_rows, sens)] + [flipped],
+        scalars=1,
     )
     back1, back0, middle = run(
         back_outer_body,
         "back_outer",
         5,
         (widened(8), widened(6), field(6, f32)),
-        [mask]
-        + [near(v) for v in (back1, back0, middle, cot_lo, cot_hi, lam_rows, sens)]
+        [spot, mask]
+        + [near(v) for v in (back1, back0, middle, cot_a, cot_b, lam_rows, sens)]
         + [flipped],
-        aliases={1: 0, 2: 1, 3: 2},
-        scalars=1,
-    )
+        aliases={2: 0, 3: 1, 4: 2},
+        scalars=2,
+    )
+    mine, others = gradient(scale, spot, (back0,), wide0, earlier)
+    beside = [(i, i ^ 1) for i in range(slabs)]
+    received = lax.ppermute(others, "slab", beside)
     coarse, average_lam = run(
         back_last_body,
         "back_last",
@@ -492,32 +510,46 @@
         [near(v) for v in (back0, middle, average_lam, factor)] + [flipped],
     )
     pieces = (groups, 128, 128)
-    mixed = gradient(scale, (back0,), wide0, 1, earlier, coarse.reshape(pieces), factor.reshape(pieces))
+    mixed = run(
+        pack_body,
+        "pack",
+        1,
+        jax.ShapeDtypeStruct((groups, 320, 128), bf16),
+        [near(v) for v in (mine, received, coarse.reshape(pieces), factor.reshape(pieces))],
+    )
     carried, shared = run(
         meet_body,
         "meet",
         1,
-        (jax.ShapeDtypeStruct(pieces, bf16), jax.ShapeDtypeStruct((slabs, 128, 128), bf16)),
+        (jax.ShapeDtypeStruct(pieces, bf16), jax.ShapeDtypeStruct((slabs // 2, 64, 128), bf16)),
         [exchanged(mixed, "tm")],
     )
+    same_core = [list(range(core, slabs, 2)) for core in range(2)]
+    shared = lax.all_to_all(shared, "slab", 0, 0, tiled=True, axis_index_groups=same_core)
     joined = run(
         join_body,
         "join",
         1,
-        jax.ShapeDtypeStruct((groups, 256, 128), bf16),
-        [exchanged(shared, "slab"), carried],
-    )
-    updated, taps, offset = run(
+        jax.ShapeDtypeStruct((groups, 192, 128), bf16),
+        [shared, carried],
+    )
+    joined = exchanged(joined, "tm")
+    received = lax.ppermute(joined[:, 128:], "slab", beside)
+    updated = run(
         finish_body,
         "finish",
-        4,
-        (
-            jax.ShapeDtypeStruct(lam.shape, f32),
-            jax.ShapeDtypeStruct(weight.shape, f32),
-            jax.ShapeDtypeStruct((1, 64), f32),
-        ),
-        [lam, average_lam, exchanged(joined, "tm")],
+        3,
+        jax.ShapeDtypeStruct(lam.shape, f32),
+        [lam, average_lam, joined],
         [TURN],
+    )
+    taps, offset = run(
+        taps_body,
+        "taps",
+        1,
+        (jax.ShapeDtypeStruct(weight.shape, f32), jax.ShapeDtypeStruct((1, 64), f32)),
+        [spot, joined, received],
+        scalars=1,
     )
     return updated[None], taps, offset[0]
 

time: 112 us -> 104 us (0.929)
  blocking collectives: 54.2 us -> 43.9 us
  Pallas kernels: 38.9 us -> 40.3 us
    all_to_all x3 -> x2, blocking collectives: 54.2 us -> 25.2 us  [exchanged(): return lax.all_to_all(value, axes, 0, 0, tiled=True)]
    all_to_all x0 -> x1, blocking collectives: none -> 18.7 us  [on_device(): lax.all_to_all(shared, 'slab', 0, 0, tiled=True, axis_index_groups=same_c...]
    pallas_call x12 -> x14, Pallas kernels: 38.9 us -> 40.3 us  [run(): pl.pallas_call(body, out_shape=outs, in_specs=in_specs, scratch_shapes=li...]
    ppermute x4 -> x6, waiting for transfers between devices: 1.94 us -> 2.78 us  [the longest x2 2.77 us: neighbours(): from_b = lax.ppermute(side_b, 'slab', across + [(j, i) for i, j in across])]
    ppermute x4 -> x6, starting transfers between devices: 12.9 us -> 13.5 us  [the longest x2 7.81 us: neighbours(): from_b = lax.ppermute(side_b, 'slab', across + [(j, i) for i, j in across])]
  transfers between devices with their start and end apart: 4 -> 6, of which waited for: 2 -> 2; matrix products, arithmetic and copies ran while one was open for 0% -> 0% of each run, Pallas kernels for 11% -> 19%
where the time goes in v3:
time: 104 us
  blocking collectives  43.9 us (42%)
  Pallas kernels  40.3 us (39%)
  starting transfers between devices  13.5 us (13%)
  waiting for transfers between devices  2.78 us (3%)
  local copies, waits for them, and re-layouts  2.25 us (2%)
    pallas_call x14, Pallas kernels, run(): pl.pallas_call(body, out_shape=outs, in_specs=in_specs, scratch_shapes=li...  40.3 us
    all_to_all x2, blocking collectives, exchanged(): return lax.all_to_all(value, axes, 0, 0, tiled=True)  25.2 us
    all_to_all x1, blocking collectives, on_device(): lax.all_to_all(shared, 'slab', 0, 0, tiled=True, axis_index_groups=same_c...  18.7 us
    ppermute x2, starting transfers between devices, neighbours(): from_b = lax.ppermute(side_b, 'slab', across + [(j, i) for i, j in across])  7.81 us
    ppermute x1, starting transfers between devices, on_device(): received = lax.ppermute(joined[:, 128:], 'slab', beside)  4.13 us
    ppermute x2, waiting for transfers between devices, neighbours(): from_b = lax.ppermute(side_b, 'slab', across + [(j, i) for i, j in across])  2.77 us
    unnamed x8, local copies, waits for them, and re-layouts  2.24 us
  transfers between devices with their start and end apart: 6, of which 2 were waited for; matrix products, arithmetic and copies ran while one was open for 0% of the time, Pallas kernels for 19%

profile of v3, /device:TPU:1, one launch (start us, length us, event | category | flops | bytes accessed | tf_op | source)
XLA Modules:
  0.0 103.7 jit_solution(7094212239827656371)
XLA Ops:
  0.6 0.0 copy-start.1
  0.7 1.2 %copy-done.1 = bf16[1,64,4,8,256]{4,3,2,1,0:T(8,128)(2,1)S(1)} copy-done((bf16[1,64,4,8,256]{4,3,2,1,0:T(8,128)(2,1)S(1)}, bf16[1,64,4,8,256]{4,3,2,1,0:T(8,128)(2,1)}, u32[]{:S(2)}) %copy-start.1) | copy-done | bytes 1048600
  1.9 0.0 copy-start.3
  1.9 1.3 %open.1 = (bf16[2,128,1024]{2,1,0:T(8,128)(2,1)}, bf16[2,128,1024]{2,1,0:T(8,128)(2,1)}) custom-call(s32[1]{0:T(128)} %bitcast.1.spot, bf16[64,4,8,256]{3,2,1,0:T(8,128)(2,1)S(1)} %bitcast.12), custom_call_target="tpu_custom_call" | custom-call | flops 3300000000 | tf_op jit(solution)/shard_map/open/pallas_call | solution.py:97
  3.1 0.0 copy-start
  3.1 1.4 %collective-permute-start = (bf16[2,128,1024]{2,1,0:T(8,128)(2,1)}, bf16[2,128,1024]{2,1,0:T(8,128)(2,1)S(1)}, u32[]{:S(2)}, u32[]{:S(2)}) collective-permute-start(bf16[2,128,1024]{2,1,0:T(8,128)(2,1)} %get-tuple-element.33.own_a), channel_id=1, source_target_pairs={{0,1},{1,0},{2,3},{3,2},{4,5},{5,4},{6,7},{7,6},{8,9},{9,8},{10,11... | collective-permute-start | bytes 1572872 | tf_op jit(solution)/shard_map/ppermute | solution.py:424
  4.6 3.6 %collective-permute-start.1 = (bf16[2,128,1024]{2,1,0:T(8,128)(2,1)}, bf16[2,128,1024]{2,1,0:T(8,128)(2,1)S(1)}, u32[]{:S(2)}, u32[]{:S(2)}) collective-permute-start(bf16[2,128,1024]{2,1,0:T(8,128)(2,1)} %get-tuple-element.34.own_b), channel_id=1, source_target_pairs={{1,2},{3,4},{5,6},{7,8},{9,10},{11,12},{13,14},{2,1},{4,3},{6,5},{... | collective-permute-start | bytes 1572872 | tf_op jit(solution)/shard_map/ppermute | solution.py:423
  8.2 0.1 pad_maximum_fusion.mask
  8.3 0.0 copy-done.3
  8.3 0.0 copy-start.2
  8.3 1.0 copy-done.2
  9.3 1.1 %prepare.1 = (bf16[256,1152]{1,0:T(8,128)(2,1)S(1)}, bf16[256,1152]{1,0:T(8,128)(2,1)S(1)}, f32[128,256]{1,0:T(8,128)S(1)}, f32[64,128]{1,0:T(8,128)S(1)}) custom-call(f32[6]{0:T(128)S(1)} %pad_maximum_fusion.mask, bf16[27,64,64]{2,1,0:T(8,128)(2,1)S(1)} %copy-done.2, f32[1,64]{1,0:T(1,128)S(1)} %bitcast.13), custom_call_target="tpu_custom_call" | custom-call | flops 2200000000 | tf_op jit(solution)/shard_map/prepare/pallas_call | solution.py:97
  10.4 0.0 copy-done
  10.4 4.7 %inner.1 = (bf16[3072,1024]{1,0:T(8,128)(2,1)S(1)}, bf16[2304,1024]{1,0:T(8,128)(2,1)S(1)}, f32[6,128,1024]{2,1,0:T(8,128)S(1)}, f32[4,128,1024]{2,1,0:T(8,128)S(1)}, f32[4,4,64,128]{3,2,1,0:T(8,128)S(1)}) custom-call(s32[1]{0:T(128)} %bitcast.1.spot, bf16[2,128,1024]{2,1,0:T(8,128)(2,1)} %get-tuple-element.33.own_a, ...), custom_call_target="tpu_custom_call" | custom-call | flops 5500000256 | tf_op jit(solution)/shard_map/inner/pallas_call | solution.py:97
  15.1 0.0 collective-permute-done.u_a
  15.1 0.1 collective-permute-done.1.u_b
  15.3 8.9 %forward.1 = (bf16[3072,1024]{1,0:T(8,128)(2,1)S(1)}, bf16[2304,1024]{1,0:T(8,128)(2,1)S(1)}, f32[6,128,1024]{2,1,0:T(8,128)S(1)}, bf16[3,128,1024]{2,1,0:T(8,12...) custom-call(s32[1]{0:T(128)} %bitcast.1.spot, ...), custom_call_target="tpu_custom_call", output_to_operand_aliasing={{0}: (2, {}), {1}: (3, {}), {2}: (4, {})} | custom-call | flops 11000000512 | tf_op jit(solution)/shard_map/forward/pallas_call | solution.py:97
  24.2 0.1 collective-permute-start.2
  24.3 4.2 %collective-permute-start.3 = (bf16[3,128,1024]{2,1,0:T(8,128)(2,1)S(1)}, bf16[3,128,1024]{2,1,0:T(8,128)(2,1)S(1)}, u32[]{:S(2)}, u32[]{:S(2)}) collective-permute-start(bf16[3,128,1024]{2,1,0:T(8,128)(2,1)S(1)} %get-tuple-element.43.own_b.refs_1_), channel_id=1, source_target_pairs={{1,2},{3,4},{5,6},{7,8},{9,10},{11,12},{13,14},{2,1},{4,3},{6,5},{... | collective-permute-start | bytes 2359304 | tf_op jit(solution)/shard_map/ppermute | solution.py:423
  28.5 2.7 %back_inner.1 = (bf16[3072,1024]{1,0:T(8,128)(2,1)S(1)}, bf16[2304,1024]{1,0:T(8,128)(2,1)S(1)}, f32[6,128,1024]{2,1,0:T(8,128)S(1)}) custom-call(s32[1]{0:T(128)} %bitcast.1.spot, bf16[3,128,1024]{2,1,0:T(8,128)(2,1)S(1)} %get-tuple-element.42.own_a.refs_0_, bf16[3,128,1024]{2,1,0:T(8,128)(2,1)S(1)} %get-tuple-element.43.own_b.refs_1_, ...), custom_call_target="tpu_custom_call" | custom-call | flops 3300000000 | tf_op jit(solution)/shard_map/back_inner/pallas_call | solution.py:97
  31.2 4.1 %gradient.2.refs_2_ = f32[16,64,128]{2,1,0:T(8,128)S(1)} custom-call(s32[1]{0:T(128)} %bitcast.1.spot, bf16[3,128,1024]{2,1,0:T(8,128)(2,1)S(1)} %get-tuple-element.42.own_a.refs_0_, bf16[3,128,1024]{2,1,0:T(8,128)(2,1)S(1)} %get-tuple-element.43.own_b.refs_1_, bf16[2304,1024]{1,0:T(8,128)(2,1)S(1)} %get-tuple-element.55.refs_2_), custom_call_target="tpu_custom_call" | custom-call | flops 5500000256 | tf_op jit(solution)/shard_map/gradient/pallas_call | solution.py:97
  35.3 0.0 collective-permute-done.2.cot_a
  35.4 2.6 %collective-permute-done.3.cot_b = bf16[3,128,1024]{2,1,0:T(8,128)(2,1)S(1)} collective-permute-done((bf16[3,128,1024]{2,1,0:T(8,128)(2,1)S(1)}, bf16[3,128,1024]{2,1,0:T(8,128)(2,1)S(1)}, u32[]{:S(2)}, u32[]{:S(2)}) %collective-permute-start.3) | collective-permute-done | bytes 786464 | tf_op jit(solution)/shard_map/ppermute | solution.py:423
  38.0 5.1 %back_outer.1 = (bf16[3072,1024]{1,0:T(8,128)(2,1)S(1)}, bf16[2304,1024]{1,0:T(8,128)(2,1)S(1)}, f32[6,128,1024]{2,1,0:T(8,128)S(1)}) custom-call(s32[1]{0:T(128)} %bitcast.1.spot, f32[6]{0:T(128)S(1)} %pad_maximum_fusion.mask, bf16[3072,1024]{1,0:T(8,128)(2,1)S(1)} %get-tuple-element.46.wide1_in, ...), custom_call_target="tpu_custom_call", output_to_operand_aliasing={{0}: (2, {}), {1}: (3, {}), {2}: (4, {})} | custom-call | flops 5500000256 | tf_op jit(solution)/shard_map/back_outer/pallas_call | solution.py:97
  43.1 4.2 %gradient.3 = (f32[8,64,128]{2,1,0:T(8,128)S(1)}, f32[8,64,128]{2,1,0:T(8,128)S(1)}) custom-call(s32[1]{0:T(128)} %bitcast.1.spot, bf16[2304,1024]{1,0:T(8,128)(2,1)S(1)} %get-tuple-element.49.wide0.refs_0_, bf16[3072,1024]{1,0:T(8,128)(2,1)S(1)} %get-tuple-element.54.refs_1_, f32[16,64,128]{2,1,0:T(8,128)S(1)} %gradient.2.refs_2_), custom_call_target="tpu_custom_call" | custom-call | flops 5500000256 | tf_op jit(solution)/shard_map/gradient/pallas_call | solution.py:97
  47.3 0.1 collective-permute-start.4
  47.4 4.4 %back_last.1 = (bf16[4,4,64,128]{3,2,1,0:T(8,128)(2,1)S(1)}, f32[4,4,64,128]{3,2,1,0:T(8,128)S(1)}) custom-call(bf16[2304,1024]{1,0:T(8,128)(2,1)S(1)} %get-tuple-element.49.wide0.refs_0_, f32[6,128,1024]{2,1,0:T(8,128)S(1)} %get-tuple-element.50.middle, f32[4,4,64,128]{3,2,1,0:T(8,128)S(1)} %get-tuple-element.51.average_lam, ...), custom_call_target="tpu_custom_call" | custom-call | flops 5500000256 | tf_op jit(solution)/shard_map/back_last/pallas_call | solution.py:97
  51.8 0.0 collective-permute-done.4.received
  51.8 0.1 pack.1
  51.9 16.0 %all_to_all.15.mixed = bf16[8,320,128]{2,1,0:T(8,128)(2,1)S(1)} all-to-all(bf16[8,320,128]{2,1,0:T(8,128)(2,1)S(1)} %pack.1), channel_id=1, replica_groups=mesh['tm'=8,'slab'=16] {'tm'}, dimensions={0} | all-to-all | bytes 1310720 | tf_op jit(solution)/shard_map/all_to_all | solution.py:429
  67.8 0.1 meet.1
  67.9 18.7 %all_to_all.16.shared = bf16[8,64,128]{2,1,0:T(8,128)(2,1)S(1)} all-to-all(bf16[8,64,128]{2,1,0:T(8,128)(2,1)S(1)} %get-tuple-element.59), channel_id=1, replica_groups={{0,2,4,6,8,10,12,14},{1,3,5,7,9,11,13,15},{16,18,20,22,24,26,28,30},{17..., dimensions={0} | all-to-all | bytes 262144 | tf_op jit(solution)/shard_map/all_to_all | solution.py:528
  86.7 9.3 %all_to_all.17.joined = bf16[8,192,128]{2,1,0:T(8,128)(2,1)S(1)} all-to-all(bf16[8,192,128]{2,1,0:T(8,128)(2,1)S(1)} %join.1), channel_id=1, replica_groups=mesh['tm'=8,'slab'=16] {'tm'}, dimensions={0} | all-to-all | bytes 786432 | tf_op jit(solution)/shard_map/all_to_all | solution.py:429
  95.9 4.1 %collective-permute-start.5 = (bf16[8,64,128]{2,1,0:T(8,128)(2,1)S(1)}, bf16[8,64,128]{2,1,0:T(8,128)(2,1)S(1)}, u32[]{:S(2)}, u32[]{:S(2)}) collective-permute-start(bf16[8,64,128]{2,1,0:T(8,128)(2,1)S(1)} %slice.4), channel_id=1, source_target_pairs={{0,1},{1,0},{2,3},{3,2},{4,5},{5,4},{6,7},{7,6},{8,9},{9,8},{10,11... | collective-permute-start | bytes 393224 | tf_op jit(solution)/shard_map/ppermute | solution.py:537
  100.1 2.6 %finish.1 = f32[64,4,8,256]{3,2,1,0:T(8,128)} custom-call(f32[64,4,8,256]{3,2,1,0:T(8,128)S(1)} %bitcast.11, f32[4,4,64,128]{3,2,1,0:T(8,128)S(1)} %get-tuple-element.53.average_lam, bf16[8,192,128]{2,1,0:T(8,128)(2,1)S(1)} %all_to_all.17.joined), custom_call_target="tpu_custom_call" | custom-call | flops 3300000000 | tf_op jit(solution)/shard_map/finish/pallas_call | solution.py:97
  102.6 0.0 collective-permute-done.5.received
  102.6 1.1 %taps.1 = (f32[27,64,64]{2,1,0:T(8,128)}, f32[1,64]{1,0:T(1,128)}) custom-call(s32[1]{0:T(128)} %bitcast.1.spot, bf16[8,192,128]{2,1,0:T(8,128)(2,1)S(1)} %all_to_all.17.joined, bf16[8,64,128]{2,1,0:T(8,128)(2,1)S(1)} %collective-permute-done.5.received), custom_call_target="tpu_custom_call" | custom-call | flops 1100000000 | tf_op jit(solution)/shard_map/taps/pallas_call | solution.py:97
  (3 shorter events, 0.0 us)
Async XLA Ops:
  0.6 1.2 %copy-start.1 = (bf16[1,64,4,8,256]{4,3,2,1,0:T(8,128)(2,1)S(1)}, bf16[1,64,4,8,256]{4,3,2,1,0:T(8,128)(2,1)}, u32[]{:S(2)}) copy-start(bf16[1,64,4,8,256]{4,3,2,1,0:T(8,128)(2,1)} %param.4) | copy-start | bytes 3145732
  1.9 6.4 %copy-start.3 = (f32[64]{0:T(128)S(1)}, f32[64]{0:T(128)}, u32[]{:S(2)}) copy-start(f32[64]{0:T(128)} %param.7) | copy-start | bytes 772
  3.1 7.2 %copy-start = (f32[1,64,4,8,256]{4,3,2,1,0:T(8,128)S(1)}, f32[1,64,4,8,256]{4,3,2,1,0:T(8,128)}, u32[]{:S(2)}) copy-start(f32[1,64,4,8,256]{4,3,2,1,0:T(8,128)} %param.5) | copy-start | bytes 6291460
  3.1 12.0 %collective-permute-start = (bf16[2,128,1024]{2,1,0:T(8,128)(2,1)}, bf16[2,128,1024]{2,1,0:T(8,128)(2,1)S(1)}, u32[]{:S(2)}, u32[]{:S(2)}) collective-permute-start(bf16[2,128,1024]{2,1,0:T(8,128)(2,1)} %get-tuple-element.33.own_a), channel_id=1, source_target_pairs={{0,1},{1,0},{2,3},{3,2},{4,5},{5,4},{6,7},{7,6},{8,9},{9,8},{10,11... | collective-permute-start | bytes 1572872 | tf_op jit(solution)/shard_map/ppermute | solution.py:424
  4.6 10.7 %collective-permute-start.1 = (bf16[2,128,1024]{2,1,0:T(8,128)(2,1)}, bf16[2,128,1024]{2,1,0:T(8,128)(2,1)S(1)}, u32[]{:S(2)}, u32[]{:S(2)}) collective-permute-start(bf16[2,128,1024]{2,1,0:T(8,128)(2,1)} %get-tuple-element.34.own_b), channel_id=1, source_target_pairs={{1,2},{3,4},{5,6},{7,8},{9,10},{11,12},{13,14},{2,1},{4,3},{6,5},{... | collective-permute-start | bytes 1572872 | tf_op jit(solution)/shard_map/ppermute | solution.py:423
  8.3 1.0 copy-start.2
  24.2 11.1 %collective-permute-start.2 = (bf16[3,128,1024]{2,1,0:T(8,128)(2,1)S(1)}, bf16[3,128,1024]{2,1,0:T(8,128)(2,1)S(1)}, u32[]{:S(2)}, u32[]{:S(2)}) collective-permute-start(bf16[3,128,1024]{2,1,0:T(8,128)(2,1)S(1)} %get-tuple-element.42.own_a.refs_0_), channel_id=1, source_target_pairs={{0,1},{1,0},{2,3},{3,2},{4,5},{5,4},{6,7},{7,6},{8,9},{9,8},{10,11... | collective-permute-start | bytes 2359304 | tf_op jit(solution)/shard_map/ppermute | solution.py:424
  24.3 13.7 %collective-permute-start.3 = (bf16[3,128,1024]{2,1,0:T(8,128)(2,1)S(1)}, bf16[3,128,1024]{2,1,0:T(8,128)(2,1)S(1)}, u32[]{:S(2)}, u32[]{:S(2)}) collective-permute-start(bf16[3,128,1024]{2,1,0:T(8,128)(2,1)S(1)} %get-tuple-element.43.own_b.refs_1_), channel_id=1, source_target_pairs={{1,2},{3,4},{5,6},{7,8},{9,10},{11,12},{13,14},{2,1},{4,3},{6,5},{... | collective-permute-start | bytes 2359304 | tf_op jit(solution)/shard_map/ppermute | solution.py:423
  47.3 4.5 %collective-permute-start.4 = (f32[8,64,128]{2,1,0:T(8,128)S(1)}, f32[8,64,128]{2,1,0:T(8,128)S(1)}, u32[]{:S(2)}, u32[]{:S(2)}) collective-permute-start(f32[8,64,128]{2,1,0:T(8,128)S(1)} %get-tuple-element.57), channel_id=1, source_target_pairs={{0,1},{1,0},{2,3},{3,2},{4,5},{5,4},{6,7},{7,6},{8,9},{9,8},{10,11... | collective-permute-start | bytes 786440 | tf_op jit(solution)/shard_map/ppermute | solution.py:504
  95.9 6.7 %collective-permute-start.5 = (bf16[8,64,128]{2,1,0:T(8,128)(2,1)S(1)}, bf16[8,64,128]{2,1,0:T(8,128)(2,1)S(1)}, u32[]{:S(2)}, u32[]{:S(2)}) collective-permute-start(bf16[8,64,128]{2,1,0:T(8,128)(2,1)S(1)} %slice.4), channel_id=1, source_target_pairs={{0,1},{1,0},{2,3},{3,2},{4,5},{5,4},{6,7},{7,6},{8,9},{9,8},{10,11... | collective-permute-start | bytes 393224 | tf_op jit(solution)/shard_map/ppermute | solution.py:537

commit v4 on v3

--- a/solution.py
+++ b/solution.py
@@ -101,7 +101,7 @@
         scratch_shapes=list(scratch),
         input_output_aliases=aliases or {},
         compiler_params=pltpu.CompilerParams(vmem_limit_bytes=limit * 2**20),
-        cost_estimate=pl.CostEstimate(flops=int(micros * 1.1e9), bytes_accessed=0, transcendentals=0),
+        cost_estimate=pl.CostEstimate(flops=int(micros * 1e8), bytes_accessed=0, transcendentals=0),
         name=name,
     )(*ins)
 
@@ -114,12 +114,27 @@
     return 2 * (1 - odd), 2 * odd
 
 
-def open_body(spot, u, out_a, out_b, turn):
-    for base, target in zip(sides(spot), (out_a, out_b)):
-        for place in range(2):
-            to_rows(u, base + place, turn)
-            for pair in range(4):
-                target[place, :, pair * 256 : pair * 256 + 256] = pair_of(turn, pair).astype(bf16)
+def open_body(side, spot, u, out, planes, turn, arrived):
+    base = sides(spot)[side]
+    copy = pltpu.make_async_copy(u.at[:, pl.ds(base, 2)], planes, arrived)
+    copy.start()
+    copy.wait()
+    for place in range(2):
+        to_rows(planes, place, turn)
+        for pair in range(4):
+            out[place, :, pair * 256 : pair * 256 + 256] = pair_of(turn, pair).astype(bf16)
+
+
+def opened(side, spot, u):
+    return pl.pallas_call(
+        functools.partial(open_body, side),
+        out_shape=field(2, bf16),
+        in_specs=[pl.BlockSpec(memory_space=pltpu.SMEM), pl.BlockSpec(memory_space=pltpu.HBM)],
+        scratch_shapes=[pltpu.VMEM((64, 2, 8, 256), bf16), TURN, pltpu.SemaphoreType.DMA(())],
+        compiler_params=pltpu.CompilerParams(vmem_limit_bytes=8 * 2**20),
+        cost_estimate=pl.CostEstimate(flops=10**8, bytes_accessed=0, transcendentals=0),
+        name="open",
+    )(spot, u)
 
 
 def put_planes(wide, z, source):
@@ -141,7 +156,7 @@
         put(wide1, z, 0, pair, value.astype(bf16))
 
 
-def inner_body(spot, own_a, own_b, lam, matrix, bias, wide0, wide1, sens, lam_rows, average_lam, turn):
+def inner_body(spot, own_a, own_b, lam, matrix, bias, wide0, wide1, sens, factor, lam_rows, average_lam, turn):
     average = averaging()
     for base, source in zip(sides(spot), (own_a, own_b)):
         put_planes(wide0, base + 2, source)
@@ -151,7 +166,7 @@
         step_state(z, matrix, offset, wide0, wide1, sens, None)
         return carry
 
-    lax.fori_loop(2, 4, inside, 0)
+    lax.fori_loop(2, 4, inside, 0, unroll=True)
     for z in range(4):
         to_rows(lam, z, turn)
         for pair in range(4):
@@ -161,37 +176,25 @@
             average_lam[z, pair] = split_dot(value[0:64] + value[64:128], average)
 
 
-def forward_body(spot, mask, wide0_in, wide1_in, sens_in, u_a, u_b, lam, matrix, bias, diag, wide0, wide1, sens, cot_a, cot_b, factor):
-    for base, source in zip(sides(spot), (u_a, u_b)):
-        put_planes(wide0, 3 * base, source)
+def forward_body(side, spot, mask, wide0_in, wide1_in, sens_in, factor_in, halo, lam, matrix, bias, diag, wide0, wide1, sens, factor, cot):
+    base = sides(spot)[side]
+    put_planes(wide0, 3 * base, halo)
     offset = bias[...]
-
-    def outside(index, carry):
-        z = index + 2 * (index // 2)
+    for place in range(2):
+        z = 2 * base + place
         step_state(z, matrix, offset, wide0, wide1, sens, mask[z])
-        return carry
-
-    lax.fori_loop(0, 4, outside, 0)
     average = averaging()
-
-    def second(z, target, place):
+    cot[2] = lam[base + base // 2].astype(bf16)
+    for place in range(2):
+        z = base + place
         parts = products(matrix, wide1, z)
         for pair in range(4):
             cols = slice(pair * 256, pair * 256 + 256)
             tanh = jnp.tanh(combined(parts, pair) + offset)
-            target[place, :, cols] = ((1.0 - tanh * tanh) * lam[z, :, cols]).astype(bf16)
+            cot[place, :, cols] = ((1.0 - tanh * tanh) * lam[z, :, cols]).astype(bf16)
             both = sens[z + 1, 0:64, cols] + sens[z + 1, 64:128, cols]
             coarse = jnp.dot(both.astype(bf16), average, preferred_element_type=f32)
             factor[z, pair] = (coarse * diag[...]).astype(bf16)
-
-    for base, target in zip(sides(spot), (cot_a, cot_b)):
-        target[2] = lam[base + base // 2].astype(bf16)
-
-        def plane(place, carry, base=base, target=target):
-            second(base + place, target, place)
-            return carry
-
-        lax.fori_loop(0, 2, plane, 0)
 
 
 def step_back(z, matrix, wide1, wide0, middle, sens, lam, weight):
@@ -214,22 +217,16 @@
         step_back(z, matrix, wide1, wide0, middle, sens, lambda cols: lam[z - 1, :, cols], None)
         return carry
 
-    lax.fori_loop(2, 4, inside, 0)
-
-
-def back_outer_body(spot, mask, wide1_in, wide0_in, middle_in, cot_a, cot_b, lam, sens, matrix, wide1, wide0, middle):
-    for base, source in zip(sides(spot), (cot_a, cot_b)):
-        put_planes(wide1, 3 * base, source)
-
-    def outside(index, carry):
-        z = 1 + 3 * index
-        step_back(z, matrix, wide1, wide0, middle, sens, lambda cols: lam[z - 1, :, cols], None)
-        return carry
-
-    lax.fori_loop(0, 2, outside, 0)
-    for base, source in zip(sides(spot), (cot_a, cot_b)):
-        z = 2 * base + base // 2
-        step_back(z, matrix, wide1, wide0, middle, sens, lambda cols: source[2, :, cols].astype(f32), mask[z])
+    lax.fori_loop(2, 4, inside, 0, unroll=True)
+
+
+def back_outer_body(side, spot, mask, wide1_in, wide0_in, middle_in, halo, lam, sens, matrix, wide1, wide0, middle):
+    base = sides(spot)[side]
+    put_planes(wide1, 3 * base, halo)
+    z = 1 + base + base // 2
+    step_back(z, matrix, wide1, wide0, middle, sens, lambda cols: lam[z - 1, :, cols], None)
+    far = 2 * base + base // 2
+    step_back(far, matrix, wide1, wide0, middle, sens, lambda cols: halo[2, :, cols].astype(f32), mask[far])
 
 
 def back_last_body(wide0, middle, average_lam, factor, matrix, coarse, kept):
@@ -282,7 +279,7 @@
         )
         return carry
 
-    lax.fori_loop(0, 4, plane, 0)
+    lax.fori_loop(0, 4, plane, 0, unroll=True)
     lower = lax.broadcasted_iota(jnp.int32, (64, 128), 1) < 64
 
     def give(block, value):
@@ -368,7 +365,7 @@
         out[:, z] = lam[:, z] + added
         return carry
 
-    lax.fori_loop(0, 4, plane, 0)
+    lax.fori_loop(0, 4, plane, 0, unroll=True)
 
 
 def taps_body(spot, joined, received, taps, offset):
@@ -417,12 +414,13 @@
     diag[...] = jnp.broadcast_to(2.0 * STEP * column(weight[13].astype(f32)), (64, 128))
 
 
-def neighbours(side_a, side_b):
-    count = lax.axis_size("slab")
-    across = [(i, i + 1) for i in range(1, count - 1, 2)]
-    from_b = lax.ppermute(side_b, "slab", across + [(j, i) for i, j in across])
-    from_a = lax.ppermute(side_a, "slab", [(i, i ^ 1) for i in range(count)])
-    return from_a, from_b
+def beside(value):
+    return lax.ppermute(value, "slab", [(i, i ^ 1) for i in range(lax.axis_size("slab"))])
+
+
+def across(value):
+    up = [(i, i + 1) for i in range(1, lax.axis_size("slab") - 1, 2)]
+    return lax.ppermute(value, "slab", up + [(j, i) for i, j in up])
 
 
 def exchanged(value, axes):
@@ -433,12 +431,13 @@
     u, lam = u_states[0], lam_points[0]
     slab, slabs = lax.axis_index("slab"), lax.axis_size("slab")
     groups = lax.axis_size("tm")
-    half = field(2, bf16)
     ones = jnp.ones((4,), f32)
     mask = jnp.concatenate([(slab > 0).astype(f32)[None], ones, (slab < slabs - 1).astype(f32)[None]])
     spot = (slab % 2).astype(jnp.int32)[None]
-    own_a, own_b = run(open_body, "open", 3, (half, half), [spot, u], [TURN], scalars=1)
-    u_a, u_b = neighbours(own_a, own_b)
+    own_b = opened(1, spot, u)
+    halo_b = across(own_b)
+    own_a = opened(0, spot, u)
+    halo_a = beside(own_a)
     taps = pltpu.VMEM((256, 1152), bf16)
     matrix, flipped, offset, diag = run(
         prepare_body,
@@ -451,33 +450,32 @@
     matrix, flipped, offset, diag = (near(v) for v in (matrix, flipped, offset, diag))
     coarse_shape = pltpu.VMEM((4, 4, 64, 128), bf16)
     average_shape = (4, 4, 64, 128)
-    wide0, wide1, sens, lam_rows, average_lam = run(
+    states = (widened(8), widened(6), field(6, f32))
+    *kept, lam_rows, average_lam = run(
         inner_body,
         "inner",
         5,
-        (
-            widened(8),
-            widened(6),
-            field(6, f32),
-            field(4, f32),
-            pltpu.VMEM(average_shape, f32),
-        ),
+        (*states, coarse_shape, field(4, f32), pltpu.VMEM(average_shape, f32)),
         [spot, near(own_a), near(own_b), lam, matrix, offset],
         [TURN],
         scalars=1,
     )
-    wide0, wide1, sens, own_a, own_b, factor = run(
-        forward_body,
-        "forward",
-        10,
-        (widened(8), widened(6), field(6, f32), field(3, bf16), field(3, bf16), coarse_shape),
-        [spot, mask]
-        + [near(v) for v in (wide0, wide1, sens, u_a, u_b, lam_rows)]
-        + [matrix, offset, diag],
-        aliases={2: 0, 3: 1, 4: 2},
-        scalars=2,
-    )
-    cot_a, cot_b = neighbours(own_a, own_b)
+
+    def forward(side, kept, halo):
+        return run(
+            functools.partial(forward_body, side),
+            "forward",
+            4,
+            (*states, coarse_shape, field(3, bf16)),
+            [spot, mask] + [near(v) for v in (*kept, halo, lam_rows)] + [matrix, offset, diag],
+            aliases={2: 0, 3: 1, 4: 2, 5: 3},
+            scalars=2,
+        )
+
+    *kept, own_a = forward(0, kept, halo_a)
+    cot_a = beside(own_a)
+    wide0, wide1, sens, factor, own_b = forward(1, kept, halo_b)
+    cot_b = across(own_b)
     scale = STEP / math.sqrt(2 * groups * slabs * 4 * 8 * 256)
     earlier = gradient(scale, spot, (own_a, own_b), wide1)
     back1, back0, middle = run(
@@ -488,20 +486,20 @@
         [spot] + [near(v) for v in (own_a, own_b, lam_rows, sens)] + [flipped],
         scalars=1,
     )
-    back1, back0, middle = run(
-        back_outer_body,
-        "back_outer",
-        5,
-        (widened(8), widened(6), field(6, f32)),
-        [spot, mask]
-        + [near(v) for v in (back1, back0, middle, cot_a, cot_b, lam_rows, sens)]
-        + [flipped],
-        aliases={2: 0, 3: 1, 4: 2},
-        scalars=2,
-    )
+    kept = (back1, back0, middle)
+    for side, halo in enumerate((cot_a, cot_b)):
+        kept = run(
+            functools.partial(back_outer_body, side),
+            "back_outer",
+            3,
+            states,
+            [spot, mask] + [near(v) for v in (*kept, halo, lam_rows, sens)] + [flipped],
+            aliases={2: 0, 3: 1, 4: 2},
+            scalars=2,
+        )
+    back1, back0, middle = kept
     mine, others = gradient(scale, spot, (back0,), wide0, earlier)
-    beside = [(i, i ^ 1) for i in range(slabs)]
-    received = lax.ppermute(others, "slab", beside)
+    received = beside(others)
     coarse, average_lam = run(
         back_last_body,
         "back_last",
@@ -534,7 +532,7 @@
         [shared, carried],
     )
     joined = exchanged(joined, "tm")
-    received = lax.ppermute(joined[:, 128:], "slab", beside)
+    received = beside(joined[:, 128:])
     updated = run(
         finish_body,
         "finish",

time: 104 us -> 98.3 us (0.945)
  Pallas kernels: 40.3 us -> 37.1 us
  waiting for transfers between devices: 2.78 us -> 1.12 us
  blocking collectives: 43.9 us -> 42.7 us
    pallas_call x14 -> x15, Pallas kernels: 40.3 us -> 36.5 us  [run(): pl.pallas_call(body, out_shape=outs, in_specs=in_specs, scratch_shapes=li...]
    ppermute x6, waiting for transfers between devices: 2.78 us -> 1.12 us  [the longest x2 1.11 us: across(): return lax.ppermute(value, 'slab', up + [(j, i) for i, j in up])]
    all_to_all x1, blocking collectives: 18.7 us -> 17.5 us  [on_device(): lax.all_to_all(shared, 'slab', 0, 0, tiled=True, axis_index_groups=same_c...]
  transfers between devices with their start and end apart: 6 -> 6, of which waited for: 2 -> 1; matrix products, arithmetic and copies ran while one was open for 0% -> 0% of each run, Pallas kernels for 19% -> 30%
where the time goes in v4:
time: 98.3 us; the launch traced here: 97.9 us
  blocking collectives  42.7 us (43%)
  Pallas kernels  37.1 us (38%)
  starting transfers between devices  13 us (13%)
  local copies, waits for them, and re-layouts  3.05 us (3%)
  waiting for transfers between devices  1.12 us (1%)
    pallas_call x15, Pallas kernels, run(): pl.pallas_call(body, out_shape=outs, in_specs=in_specs, scratch_shapes=li...  36.5 us
    all_to_all x2, blocking collectives, exchanged(): return lax.all_to_all(value, axes, 0, 0, tiled=True)  25.2 us
    all_to_all x1, blocking collectives, on_device(): lax.all_to_all(shared, 'slab', 0, 0, tiled=True, axis_index_groups=same_c...  17.5 us
    ppermute x2, starting transfers between devices, across(): return lax.ppermute(value, 'slab', up + [(j, i) for i, j in up])  7.62 us
    ppermute x4, starting transfers between devices, beside(): lax.ppermute(value, 'slab', [(i, i ^ 1) for i in range(lax.axis_size('sla...  5.41 us
    unnamed x8, local copies, waits for them, and re-layouts  3.04 us
  transfers between devices with their start and end apart: 6, of which 1 were waited for; matrix products, arithmetic and copies ran while one was open for 0% of the time, Pallas kernels for 30%

profile of v4, /device:TPU:1, one launch (start us, length us, event | category | flops | bytes accessed | tf_op | source)
XLA Modules:
  0.0 97.9 jit_solution(3197149577960840931)
XLA Ops:
  0.6 0.0 copy-start
  0.7 0.0 copy-start.1
  0.7 1.4 %copy-done.1 = bf16[1,64,4,8,256]{4,3,2,1,0:T(8,128)(2,1)S(1)} copy-done((bf16[1,64,4,8,256]{4,3,2,1,0:T(8,128)(2,1)S(1)}, bf16[1,64,4,8,256]{4,3,2,1,0:T(8,128)(2,1)}, u32[]{:S(2)}) %copy-start.1) | copy-done | bytes 1048600
  2.0 0.3 open.2.own_a
  2.4 1.5 %collective-permute-start = (bf16[2,128,1024]{2,1,0:T(8,128)(2,1)S(1)}, bf16[2,128,1024]{2,1,0:T(8,128)(2,1)}, u32[]{:S(2)}, u32[]{:S(2)}) collective-permute-start(bf16[2,128,1024]{2,1,0:T(8,128)(2,1)S(1)} %open.2.own_a), channel_id=1, source_target_pairs={{0,1},{1,0},{2,3},{3,2},{4,5},{5,4},{6,7},{7,6},{8,9},{9,8},{10,11... | collective-permute-start | bytes 1572872 | tf_op jit(solution)/shard_map/ppermute | solution.py:418
  3.9 0.3 open.3.own_b
  4.2 3.5 %collective-permute-start.1 = (bf16[2,128,1024]{2,1,0:T(8,128)(2,1)S(1)}, bf16[2,128,1024]{2,1,0:T(8,128)(2,1)}, u32[]{:S(2)}, u32[]{:S(2)}) collective-permute-start(bf16[2,128,1024]{2,1,0:T(8,128)(2,1)S(1)} %open.3.own_b), channel_id=1, source_target_pairs={{1,2},{3,4},{5,6},{7,8},{9,10},{11,12},{13,14},{2,1},{4,3},{6,5},{... | collective-permute-start | bytes 1572872 | tf_op jit(solution)/shard_map/ppermute | solution.py:423
  7.7 0.1 pad_maximum_fusion.mask
  7.8 0.0 copy-start.2
  7.8 1.0 %copy-done.2 = bf16[27,64,64]{2,1,0:T(8,128)(2,1)S(1)} copy-done((bf16[27,64,64]{2,1,0:T(8,128)(2,1)S(1)}, bf16[27,64,64]{2,1,0:T(8,128)(2,1)}, u32[]{:S(2)}) %copy-start.2) | copy-done | bytes 221208
  8.8 0.0 copy-start.3
  8.8 0.7 copy-done.3
  9.5 1.1 %prepare.1 = (bf16[256,1152]{1,0:T(8,128)(2,1)S(1)}, bf16[256,1152]{1,0:T(8,128)(2,1)S(1)}, f32[128,256]{1,0:T(8,128)S(1)}, f32[64,128]{1,0:T(8,128)S(1)}) custom-call(f32[6]{0:T(128)S(1)} %pad_maximum_fusion.mask, bf16[27,64,64]{2,1,0:T(8,128)(2,1)S(1)} %copy-done.2, f32[1,64]{1,0:T(1,128)S(1)} %bitcast.16), custom_call_target="tpu_custom_call" | custom-call | flops 200000000 | tf_op jit(solution)/shard_map/prepare/pallas_call | solution.py:97
  10.6 0.0 copy-done
  10.6 3.1 %inner.1 = (bf16[3072,1024]{1,0:T(8,128)(2,1)S(1)}, bf16[2304,1024]{1,0:T(8,128)(2,1)S(1)}, f32[6,128,1024]{2,1,0:T(8,128)S(1)}, bf16[4,4,64,128]{3,2,1,0:T(8,12...) custom-call(s32[1]{0:T(128)} %bitcast.1.spot, bf16[2,128,1024]{2,1,0:T(8,128)(2,1)S(1)} %open.2.own_a, ...), custom_call_target="tpu_custom_call" | custom-call | flops 500000000 | tf_op jit(solution)/shard_map/inner/pallas_call | solution.py:97
  13.7 0.0 collective-permute-done.halo
  13.7 5.2 %forward.2 = (bf16[3072,1024]{1,0:T(8,128)(2,1)S(1)}, bf16[2304,1024]{1,0:T(8,128)(2,1)S(1)}, f32[6,128,1024]{2,1,0:T(8,128)S(1)}, bf16[4,4,64,128]{3,2,1,0:T(8,128)(2,1)S(1)}, bf16[3,128,1024]{2,1,0:T(8,128)(2,1)S(1)}) custom-call(s32[1]{0:T(128)} %bitcast.1.spot, ...), custom_call_target="tpu_custom_call", output_to_operand_aliasing={{0}: (2, {}), {1}: (3, {}), {2}: (4, {}), {3}: (5, {})} | custom-call | flops 400000000 | tf_op jit(solution)/shard_map/forward/pallas_call | solution.py:97
  18.9 0.1 collective-permute-start.2
  19.0 0.0 collective-permute-done.1.halo
  19.0 5.2 %forward.3 = (bf16[3072,1024]{1,0:T(8,128)(2,1)S(1)}, bf16[2304,1024]{1,0:T(8,128)(2,1)S(1)}, f32[6,128,1024]{2,1,0:T(8,128)S(1)}, bf16[4,4,64,128]{3,2,1,0:T(8,128)(2,1)S(1)}, bf16[3,128,1024]{2,1,0:T(8,128)(2,1)S(1)}) custom-call(s32[1]{0:T(128)} %bitcast.1.spot, ...), custom_call_target="tpu_custom_call", output_to_operand_aliasing={{0}: (2, {}), {1}: (3, {}), {2}: (4, {}), {3}: (5, {})} | custom-call | flops 400000000 | tf_op jit(solution)/shard_map/forward/pallas_call | solution.py:97
  24.2 4.1 %collective-permute-start.3 = (bf16[3,128,1024]{2,1,0:T(8,128)(2,1)S(1)}, bf16[3,128,1024]{2,1,0:T(8,128)(2,1)S(1)}, u32[]{:S(2)}, u32[]{:S(2)}) collective-permute-start(bf16[3,128,1024]{2,1,0:T(8,128)(2,1)S(1)} %get-tuple-element.52.own_b.refs_1_), channel_id=1, source_target_pairs={{1,2},{3,4},{5,6},{7,8},{9,10},{11,12},{13,14},{2,1},{4,3},{6,5},{... | collective-permute-start | bytes 2359304 | tf_op jit(solution)/shard_map/ppermute | solution.py:423
  28.3 2.4 %back_inner.1 = (bf16[3072,1024]{1,0:T(8,128)(2,1)S(1)}, bf16[2304,1024]{1,0:T(8,128)(2,1)S(1)}, f32[6,128,1024]{2,1,0:T(8,128)S(1)}) custom-call(s32[1]{0:T(128)} %bitcast.1.spot, bf16[3,128,1024]{2,1,0:T(8,128)(2,1)S(1)} %get-tuple-element.47.own_a.refs_0_, bf16[3,128,1024]{2,1,0:T(8,128)(2,1)S(1)} %get-tuple-element.52.own_b.refs_1_, ...), custom_call_target="tpu_custom_call" | custom-call | flops 300000000 | tf_op jit(solution)/shard_map/back_inner/pallas_call | solution.py:97
  30.7 3.0 %gradient.2.refs_2_ = f32[16,64,128]{2,1,0:T(8,128)S(1)} custom-call(s32[1]{0:T(128)} %bitcast.1.spot, bf16[3,128,1024]{2,1,0:T(8,128)(2,1)S(1)} %get-tuple-element.47.own_a.refs_0_, bf16[3,128,1024]{2,1,0:T(8,128)(2,1)S(1)} %get-tuple-element.52.own_b.refs_1_, bf16[2304,1024]{1,0:T(8,128)(2,1)S(1)} %get-tuple-element.67.refs_2_), custom_call_target="tpu_custom_call" | custom-call | flops 500000000 | tf_op jit(solution)/shard_map/gradient/pallas_call | solution.py:97
  33.8 0.0 collective-permute-done.2.halo
  33.8 2.9 %back_outer.2 = (bf16[3072,1024]{1,0:T(8,128)(2,1)S(1)}, bf16[2304,1024]{1,0:T(8,128)(2,1)S(1)}, f32[6,128,1024]{2,1,0:T(8,128)S(1)}) custom-call(s32[1]{0:T(128)} %bitcast.1.spot, f32[6]{0:T(128)S(1)} %pad_maximum_fusion.mask, bf16[3072,1024]{1,0:T(8,128)(2,1)S(1)} %get-tuple-element.55.wide1_in, ...), custom_call_target="tpu_custom_call", output_to_operand_aliasing={{0}: (2, {}), {1}: (3, {}), {2}: (4, {})} | custom-call | flops 300000000 | tf_op jit(solution)/shard_map/back_outer/pallas_call | solution.py:97
  36.6 1.1 %collective-permute-done.3.halo = bf16[3,128,1024]{2,1,0:T(8,128)(2,1)S(1)} collective-permute-done((bf16[3,128,1024]{2,1,0:T(8,128)(2,1)S(1)}, bf16[3,128,1024]{2,1,0:T(8,128)(2,1)S(1)}, u32[]{:S(2)}, u32[]{:S(2)}) %collective-permute-start.3) | collective-permute-done | bytes 786464 | tf_op jit(solution)/shard_map/ppermute | solution.py:423
  37.7 2.9 %back_outer.3 = (bf16[3072,1024]{1,0:T(8,128)(2,1)S(1)}, bf16[2304,1024]{1,0:T(8,128)(2,1)S(1)}, f32[6,128,1024]{2,1,0:T(8,128)S(1)}) custom-call(s32[1]{0:T(128)} %bitcast.1.spot, f32[6]{0:T(128)S(1)} %pad_maximum_fusion.mask, bf16[3072,1024]{1,0:T(8,128)(2,1)S(1)} %get-tuple-element.58.wide1_in, ...), custom_call_target="tpu_custom_call", output_to_operand_aliasing={{0}: (2, {}), {1}: (3, {}), {2}: (4, {})} | custom-call | flops 300000000 | tf_op jit(solution)/shard_map/back_outer/pallas_call | solution.py:97
  40.6 3.1 %gradient.3 = (f32[8,64,128]{2,1,0:T(8,128)S(1)}, f32[8,64,128]{2,1,0:T(8,128)S(1)}) custom-call(s32[1]{0:T(128)} %bitcast.1.spot, bf16[2304,1024]{1,0:T(8,128)(2,1)S(1)} %get-tuple-element.61.wide0.refs_0_, bf16[3072,1024]{1,0:T(8,128)(2,1)S(1)} %get-tuple-element.66.refs_1_, f32[16,64,128]{2,1,0:T(8,128)S(1)} %gradient.2.refs_2_), custom_call_target="tpu_custom_call" | custom-call | flops 500000000 | tf_op jit(solution)/shard_map/gradient/pallas_call | solution.py:97
  43.7 0.1 collective-permute-start.4
  43.8 4.4 %back_last.1 = (bf16[4,4,64,128]{3,2,1,0:T(8,128)(2,1)S(1)}, f32[4,4,64,128]{3,2,1,0:T(8,128)S(1)}) custom-call(bf16[2304,1024]{1,0:T(8,128)(2,1)S(1)} %get-tuple-element.61.wide0.refs_0_, f32[6,128,1024]{2,1,0:T(8,128)S(1)} %get-tuple-element.62.middle, f32[4,4,64,128]{3,2,1,0:T(8,128)S(1)} %get-tuple-element.63.average_lam, ...), custom_call_target="tpu_custom_call" | custom-call | flops 500000000 | tf_op jit(solution)/shard_map/back_last/pallas_call | solution.py:97
  48.1 0.0 collective-permute-done.4.received
  48.2 0.1 pack.1
  48.2 16.0 %all_to_all.15.mixed = bf16[8,320,128]{2,1,0:T(8,128)(2,1)S(1)} all-to-all(bf16[8,320,128]{2,1,0:T(8,128)(2,1)S(1)} %pack.1), channel_id=1, replica_groups=mesh['tm'=8,'slab'=16] {'tm'}, dimensions={0} | all-to-all | bytes 1310720 | tf_op jit(solution)/shard_map/all_to_all | solution.py:427
  64.2 0.1 meet.1
  64.3 17.5 %all_to_all.16.shared = bf16[8,64,128]{2,1,0:T(8,128)(2,1)S(1)} all-to-all(bf16[8,64,128]{2,1,0:T(8,128)(2,1)S(1)} %get-tuple-element.71), channel_id=1, replica_groups={{0,2,4,6,8,10,12,14},{1,3,5,7,9,11,13,15},{16,18,20,22,24,26,28,30},{17..., dimensions={0} | all-to-all | bytes 262144 | tf_op jit(solution)/shard_map/all_to_all | solution.py:526
  81.8 9.3 %all_to_all.17.joined = bf16[8,192,128]{2,1,0:T(8,128)(2,1)S(1)} all-to-all(bf16[8,192,128]{2,1,0:T(8,128)(2,1)S(1)} %join.1), channel_id=1, replica_groups=mesh['tm'=8,'slab'=16] {'tm'}, dimensions={0} | all-to-all | bytes 786432 | tf_op jit(solution)/shard_map/all_to_all | solution.py:427
  91.1 3.7 %collective-permute-start.5 = (bf16[8,64,128]{2,1,0:T(8,128)(2,1)S(1)}, bf16[8,64,128]{2,1,0:T(8,128)(2,1)S(1)}, u32[]{:S(2)}, u32[]{:S(2)}) collective-permute-start(bf16[8,64,128]{2,1,0:T(8,128)(2,1)S(1)} %slice.4), channel_id=1, source_target_pairs={{0,1},{1,0},{2,3},{3,2},{4,5},{5,4},{6,7},{7,6},{8,9},{9,8},{10,11... | collective-permute-start | bytes 393224 | tf_op jit(solution)/shard_map/ppermute | solution.py:418
  94.8 2.1 %finish.1 = f32[64,4,8,256]{3,2,1,0:T(8,128)} custom-call(f32[64,4,8,256]{3,2,1,0:T(8,128)S(1)} %bitcast.11, f32[4,4,64,128]{3,2,1,0:T(8,128)S(1)} %get-tuple-element.65.average_lam, bf16[8,192,128]{2,1,0:T(8,128)(2,1)S(1)} %all_to_all.17.joined), custom_call_target="tpu_custom_call" | custom-call | flops 300000000 | tf_op jit(solution)/shard_map/finish/pallas_call | solution.py:97
  96.9 0.0 collective-permute-done.5.received
  96.9 1.1 %taps.1 = (f32[27,64,64]{2,1,0:T(8,128)}, f32[1,64]{1,0:T(1,128)}) custom-call(s32[1]{0:T(128)} %bitcast.1.spot, bf16[8,192,128]{2,1,0:T(8,128)(2,1)S(1)} %all_to_all.17.joined, bf16[8,64,128]{2,1,0:T(8,128)(2,1)S(1)} %collective-permute-done.5.received), custom_call_target="tpu_custom_call" | custom-call | flops 100000000 | tf_op jit(solution)/shard_map/taps/pallas_call | solution.py:97
  (3 shorter events, 0.0 us)
Async XLA Ops:
  0.6 9.9 %copy-start = (f32[1,64,4,8,256]{4,3,2,1,0:T(8,128)S(1)}, f32[1,64,4,8,256]{4,3,2,1,0:T(8,128)}, u32[]{:S(2)}) copy-start(f32[1,64,4,8,256]{4,3,2,1,0:T(8,128)} %param.5) | copy-start | bytes 6291460
  0.7 1.4 %copy-start.1 = (bf16[1,64,4,8,256]{4,3,2,1,0:T(8,128)(2,1)S(1)}, bf16[1,64,4,8,256]{4,3,2,1,0:T(8,128)(2,1)}, u32[]{:S(2)}) copy-start(bf16[1,64,4,8,256]{4,3,2,1,0:T(8,128)(2,1)} %param.4) | copy-start | bytes 3145732
  2.4 11.4 %collective-permute-start = (bf16[2,128,1024]{2,1,0:T(8,128)(2,1)S(1)}, bf16[2,128,1024]{2,1,0:T(8,128)(2,1)}, u32[]{:S(2)}, u32[]{:S(2)}) collective-permute-start(bf16[2,128,1024]{2,1,0:T(8,128)(2,1)S(1)} %open.2.own_a), channel_id=1, source_target_pairs={{0,1},{1,0},{2,3},{3,2},{4,5},{5,4},{6,7},{7,6},{8,9},{9,8},{10,11... | collective-permute-start | bytes 1572872 | tf_op jit(solution)/shard_map/ppermute | solution.py:418
  4.2 14.8 %collective-permute-start.1 = (bf16[2,128,1024]{2,1,0:T(8,128)(2,1)S(1)}, bf16[2,128,1024]{2,1,0:T(8,128)(2,1)}, u32[]{:S(2)}, u32[]{:S(2)}) collective-permute-start(bf16[2,128,1024]{2,1,0:T(8,128)(2,1)S(1)} %open.3.own_b), channel_id=1, source_target_pairs={{1,2},{3,4},{5,6},{7,8},{9,10},{11,12},{13,14},{2,1},{4,3},{6,5},{... | collective-permute-start | bytes 1572872 | tf_op jit(solution)/shard_map/ppermute | solution.py:423
  7.8 1.0 %copy-start.2 = (bf16[27,64,64]{2,1,0:T(8,128)(2,1)S(1)}, bf16[27,64,64]{2,1,0:T(8,128)(2,1)}, u32[]{:S(2)}) copy-start(bf16[27,64,64]{2,1,0:T(8,128)(2,1)} %weight.1) | copy-start | bytes 663556
  8.8 0.7 copy-start.3
  18.9 14.9 %collective-permute-start.2 = (bf16[3,128,1024]{2,1,0:T(8,128)(2,1)S(1)}, bf16[3,128,1024]{2,1,0:T(8,128)(2,1)S(1)}, u32[]{:S(2)}, u32[]{:S(2)}) collective-permute-start(bf16[3,128,1024]{2,1,0:T(8,128)(2,1)S(1)} %get-tuple-element.47.own_a.refs_0_), channel_id=1, source_target_pairs={{0,1},{1,0},{2,3},{3,2},{4,5},{5,4},{6,7},{7,6},{8,9},{9,8},{10,11... | collective-permute-start | bytes 2359304 | tf_op jit(solution)/shard_map/ppermute | solution.py:418
  24.2 13.6 %collective-permute-start.3 = (bf16[3,128,1024]{2,1,0:T(8,128)(2,1)S(1)}, bf16[3,128,1024]{2,1,0:T(8,128)(2,1)S(1)}, u32[]{:S(2)}, u32[]{:S(2)}) collective-permute-start(bf16[3,128,1024]{2,1,0:T(8,128)(2,1)S(1)} %get-tuple-element.52.own_b.refs_1_), channel_id=1, source_target_pairs={{1,2},{3,4},{5,6},{7,8},{9,10},{11,12},{13,14},{2,1},{4,3},{6,5},{... | collective-permute-start | bytes 2359304 | tf_op jit(solution)/shard_map/ppermute | solution.py:423
  43.7 4.5 %collective-permute-start.4 = (f32[8,64,128]{2,1,0:T(8,128)S(1)}, f32[8,64,128]{2,1,0:T(8,128)S(1)}, u32[]{:S(2)}, u32[]{:S(2)}) collective-permute-start(f32[8,64,128]{2,1,0:T(8,128)S(1)} %get-tuple-element.69), channel_id=1, source_target_pairs={{0,1},{1,0},{2,3},{3,2},{4,5},{5,4},{6,7},{7,6},{8,9},{9,8},{10,11... | collective-permute-start | bytes 786440 | tf_op jit(solution)/shard_map/ppermute | solution.py:418
  91.1 5.8 %collective-permute-start.5 = (bf16[8,64,128]{2,1,0:T(8,128)(2,1)S(1)}, bf16[8,64,128]{2,1,0:T(8,128)(2,1)S(1)}, u32[]{:S(2)}, u32[]{:S(2)}) collective-permute-start(bf16[8,64,128]{2,1,0:T(8,128)(2,1)S(1)} %slice.4), channel_id=1, source_target_pairs={{0,1},{1,0},{2,3},{3,2},{4,5},{5,4},{6,7},{7,6},{8,9},{9,8},{10,11... | collective-permute-start | bytes 393224 | tf_op jit(solution)/shard_map/ppermute | solution.py:418
